TPU v7x, 128 devices: a whole 4x4x4 slice. The times are simulated.
128 devices in a mesh: dp: 16 (over x_hi, z, core), owner: 8 (over y, x_lo).
Axes of the slice: x: 4 (x_hi: 2, x_lo: 2; x = x_hi * 2 + x_lo), y: 4, z: 4, core: 2. Of those that a mesh axis runs over, the one named last changes fastest.
Arguments:
- inputs: bfloat16 [8192, 6144], P('dp'), may hold values from -6 to 6
- out_grads: bfloat16 [8192, 6144], P('dp'), may hold values from -6 to 6
- kernel_grad: bfloat16 [6144, 6144], P('dp', 'owner'), may hold values from -6 to 6
- basis_in: bfloat16 [6144, 6144], P(('dp', 'owner')), may hold values from -0.078125 to 0.078125
- basis_out: bfloat16 [6144, 768], P('owner'), may hold values from -0.21875 to 0.21875
- eigen_in: float32 [6144], P('dp'), may hold values from 0.3 to 3
- eigen_out: float32 [6144], P('owner'), may hold values from 0.3 to 3
- old_in_factor: float32 [6144, 6144], P('dp', 'owner'), may hold values from -0.4 to 2.4, as said below
- old_out_factor: float32 [6144, 768], P(('owner', 'dp')), may hold values from -0.4 to 2.4, as said below
Outputs:
- precond: bfloat16 [6144, 6144], P(None, 'owner')
- in_factor: float32 [6144, 6144], P('dp', 'owner')
- out_factor: float32 [6144, 768], P(('owner', 'dp'))
Inputs may be any that keep to these rules, and one draw needn't show every extreme that they name: `old_in_factor`: Symmetric, with a positive diagonal. `old_out_factor`: each block is symmetric, with a positive diagonal.
All inputs are finite; a program needn't handle non-finite values.
Results may differ from a plain program's by a relative error of at most 0.015.
Values may be sent and summed in bfloat16 or wider, within the bound.
A program may use at most 128 MiB of HBM per device.

v0:
```python
import jax
import jax.numpy as jnp
from jax import lax
from jax.sharding import PartitionSpec as P

damping = 0.3
factor_decay = 0.9


def shards(
    inputs,
    out_grads,
    kernel_grad,
    basis_in,
    basis_out,
    eigen_in,
    eigen_out,
    old_in_factor,
    old_out_factor,
):
    block_width = basis_out.shape[1]
    data_count = lax.axis_size("dp")
    total_tokens = inputs.shape[0] * data_count
    owner_index = lax.axis_index("owner")
    columns = lax.dynamic_slice_in_dim(inputs, owner_index * block_width, block_width, 1)
    in_cov = lax.psum_scatter(
        lax.dot_general(
            inputs, columns, (((0,), (0,)), ((), ())), preferred_element_type=jnp.float32
        ).astype(jnp.bfloat16),
        "dp",
        scatter_dimension=0,
        tiled=True,
    ).astype(jnp.float32)
    grad_columns = lax.dynamic_slice_in_dim(out_grads, owner_index * block_width, block_width, 1)
    out_cov = lax.psum_scatter(
        lax.dot_general(
            grad_columns, grad_columns, (((0,), (0,)), ((), ())), preferred_element_type=jnp.float32
        ).astype(jnp.bfloat16),
        "dp",
        scatter_dimension=0,
        tiled=True,
    ).astype(jnp.float32)
    in_factor = factor_decay * old_in_factor + (1.0 - factor_decay) * in_cov / total_tokens
    out_factor = factor_decay * old_out_factor + (1.0 - factor_decay) * out_cov / total_tokens
    in_factor, out_factor = (in_factor, out_factor)
    rows_basis = lax.all_gather(basis_in, "owner", axis=0, tiled=True)
    turned = jnp.dot(kernel_grad, basis_out, preferred_element_type=jnp.float32).astype(
        jnp.bfloat16
    )
    section = rows_basis
    rotated = lax.psum_scatter(
        lax.dot_general(
            section, turned, (((0,), (0,)), ((), ())), preferred_element_type=jnp.float32
        ).astype(jnp.bfloat16),
        "dp",
        scatter_dimension=0,
        tiled=True,
    ).astype(jnp.float32)
    scaled = (rotated / (eigen_in[:, None] * eigen_out[None, :] + damping)).astype(jnp.bfloat16)
    section = rows_basis
    restored = jnp.dot(
        section,
        lax.all_gather(scaled, "dp", axis=0, tiled=True),
        preferred_element_type=jnp.float32,
    )
    restored = restored.astype(jnp.bfloat16)
    local_update = lax.dot_general(
        restored, basis_out, (((1,), (1,)), ((), ())), preferred_element_type=jnp.float32
    ).astype(jnp.bfloat16)
    precond = lax.all_gather(local_update, "dp", axis=0, tiled=True)
    return (precond, in_factor, out_factor)


def solution(mesh):
    in_specs = (
        P("dp", None),
        P("dp", None),
        P("dp", "owner"),
        P(("dp", "owner"), None),
        P("owner", None),
        P("dp"),
        P("owner"),
        P("dp", "owner"),
        P(("owner", "dp"), None),
    )
    out_specs = (P(None, "owner"), P("dp", "owner"), P(("owner", "dp"), None))
    return jax.shard_map(shards, mesh=mesh, in_specs=in_specs, out_specs=out_specs, check_vma=False)
```

profile of v0, /device:TPU:1, one launch (start us, length us, event | category | flops | bytes accessed | tf_op | source)
XLA Modules:
  0.0 604.0 jit_solution(3413181560381422535)
XLA Ops:
  7.2 0.0 copy-start
  7.2 0.0 all-gather.4.cloned.1.call-start
  7.2 0.7 all-gather.4.cloned.1.call-update
  7.9 0.0 reduce-scatter.10.cloned.1.call-start
  8.0 105.1 %all-gather.4.cloned.1.call-done = bf16[384,6144]{1,0:T(8,128)(2,1)} async-done(((bf16[48,6144]{1,0:T(8,128)(2,1)}), bf16[384,6144]{1,0:T(8,128)(2,1)}) %all-gather.4.cloned.1.call-update) | async-done | bytes 4718608 | tf_op jit(solution)/shard_map/all_gather | solution.py:46
  113.1 0.0 copy-done
  113.1 10.9 %fusion.1 = bf16[6144,768]{0,1:T(8,128)(2,1)} fusion(bf16[384,6144]{1,0:T(8,128)(2,1)} %all-gather.4.cloned.1.call-done, bf16[384,768]{1,0:T(8,128)(2,1)} %param.11, bf16[768,768]{1,0:T(8,128)(2,1)S(1)} %copy-done), kind=kOutput, calls=%fused_computation.3 | convolution fusion | flops 4081876992 | bytes 15925248 | tf_op jit(solution)/shard_map/dot_general | solution.py:52
  124.0 12.7 %copy.16 = bf16[6144,768]{1,0:T(8,128)(2,1)} copy(bf16[6144,768]{0,1:T(8,128)(2,1)} %fusion.1) | data formatting | bytes 18874368
  136.7 0.0 copy-start.2
  136.7 0.0 copy-start.3
  136.7 0.0 reduce-scatter.10.cloned.1.call-update
  136.7 0.0 all-gather.6.cloned.1.call-start
  136.8 106.9 %reduce-scatter.10.cloned.1.call-done = bf16[384,768]{1,0:T(8,128)(2,1)} async-done(((bf16[6144,768]{1,0:T(8,128)(2,1)}), bf16[384,768]{1,0:T(8,128)(2,1)}) %reduce-scatter.10.cloned.1.call-update) | async-done | bytes 589840
  243.7 1.4 copy.17
  245.0 0.0 copy-done.2
  245.0 0.0 copy-done.3
  245.1 1.1 divide_convert_fusion
  246.2 0.0 all-gather.6.cloned.1.call-update
  246.2 0.0 reduce-scatter.8.cloned.1.call-start
  246.3 3.3 convolution_convert_fusion.2
  249.5 0.0 reduce-scatter.8.cloned.1.call-update
  249.5 0.0 reduce-scatter.12.cloned.1.call-start
  249.6 9.6 %fusion = bf16[6144,768]{0,1:T(8,128)(2,1)} fusion(bf16[512,6144]{1,0:T(8,128)(2,1)} %param.9, s32[]{:T(128)S(6)} %select_n.4), kind=kOutput, calls=%fused_computation.2 | convolution fusion | flops 4836556800 | bytes 16515076 | tf_op jit(solution)/shard_map/dot_general | solution.py:27
  259.2 12.7 %copy.18 = bf16[6144,768]{1,0:T(8,128)(2,1)} copy(bf16[6144,768]{0,1:T(8,128)(2,1)} %fusion) | data formatting | bytes 18874368
  271.9 0.0 reduce-scatter.12.cloned.1.call-update
  272.0 0.0 copy-start.1
  272.0 0.2 all-gather.8.cloned.1.call-start
  272.2 56.7 %all-gather.6.cloned.1.call-done = bf16[6144,768]{0,1:T(8,128)(2,1)} async-done(((bf16[384,768]{0,1:T(8,128)(2,1)}), bf16[6144,768]{0,1:T(8,128)(2,1)}) %all-gather.6.cloned.1.call-update) | async-done | bytes 9437200 | tf_op jit(solution)/shard_map/all_gather | solution.py:63
  328.9 11.7 %convolution_convert_fusion.3 = bf16[384,768]{1,0:T(8,128)(2,1)} fusion(bf16[768,768]{1,0:T(8,128)(2,1)S(1)} %copy-done, bf16[6144,768]{0,1:T(8,128)(2,1)} %all-gather.6.cloned.1.call-done, bf16[384,6144]{1,0:T(8,128)(2,1)} %all-gather.4.cloned.1.call-done), kind=kOutput, calls=%fused_computation.5 | convolution fusion | flops 4077453312 | bytes 15925248 | tf_op jit(solution)/shard_map/dot_general | solution.py:67
  340.5 0.0 all-gather.8.cloned.1.call-update
  340.5 0.0 copy-done.1
  340.6 0.4 copy.14
  340.9 55.5 %reduce-scatter.8.cloned.1.call-done = bf16[48,768]{1,0:T(8,128)(2,1)} async-done(((bf16[768,768]{1,0:T(8,128)(2,1)}), bf16[48,768]{1,0:T(8,128)(2,1)}) %reduce-scatter.8.cloned.1.call-update) | async-done | bytes 73744 | tf_op jit(solution)/shard_map/reduce_scatter | solution.py:35
  396.4 1.6 multiply_add_fusion.1
  398.0 110.5 %reduce-scatter.12.cloned.1.call-done = bf16[384,768]{1,0:T(8,128)(2,1)} async-done(((bf16[6144,768]{1,0:T(8,128)(2,1)}), bf16[384,768]{1,0:T(8,128)(2,1)}) %reduce-scatter.12.cloned.1.call-update) | async-done | bytes 589840
  508.6 2.1 copy.19
  510.7 1.2 multiply_add_fusion
  511.9 1.4 copy.15
  513.3 75.8 %all-gather.8.cloned.1.call-done = bf16[6144,768]{1,0:T(8,128)(2,1)} async-done(((bf16[384,768]{1,0:T(8,128)(2,1)}), bf16[6144,768]{1,0:T(8,128)(2,1)}) %all-gather.8.cloned.1.call-update) | async-done | bytes 9437200 | tf_op jit(solution)/shard_map/all_gather | solution.py:70
  589.1 8.0 %copy.21 = bf16[6144,768]{1,0:T(8,128)(2,1)} copy(bf16[6144,768]{1,0:T(8,128)(2,1)} %all-gather.8.cloned.1.call-done) | data formatting | bytes 18874368
Async XLA Ops:
  7.2 105.9 %copy-start = (bf16[768,768]{1,0:T(8,128)(2,1)S(1)}, bf16[768,768]{1,0:T(8,128)(2,1)}, u32[]{:S(2)}) copy-start(bf16[768,768]{1,0:T(8,128)(2,1)} %param.13) | copy-start | bytes 3538948
  7.2 105.9 %all-gather.4.cloned.1.call-start = ((), (), s32[]{:S(2)}) async-start(), calls=%async_computation.3 | async-start | bytes 5308416 | tf_op jit(solution)/shard_map/all_gather | solution.py:46
  7.9 235.7 %reduce-scatter.10.cloned.1.call-start = ((), (), s32[]{:S(2)}) async-start(), calls=%async_computation.7 | async-start | bytes 10027008
  136.7 108.3 %copy-start.2 = (f32[768]{0:T(1024)S(1)}, f32[768]{0:T(1024)}, u32[]{:S(2)}) copy-start(f32[768]{0:T(1024)} %param.15) | copy-start | bytes 9220
  136.7 108.3 %copy-start.3 = (f32[384]{0:T(512)S(1)}, f32[384]{0:T(512)}, u32[]{:S(2)}) copy-start(f32[384]{0:T(512)} %param.14) | copy-start | bytes 4612
  136.7 192.1 %all-gather.6.cloned.1.call-start = ((), (), s32[]{:S(2)}) async-start(), calls=%async_computation.4 | async-start | bytes 10027008 | tf_op jit(solution)/shard_map/all_gather | solution.py:63
  246.2 150.2 %reduce-scatter.8.cloned.1.call-start = ((), (), s32[]{:S(2)}) async-start(), calls=%async_computation.6 | async-start | bytes 1253376 | tf_op jit(solution)/shard_map/reduce_scatter | solution.py:35
  249.5 259.0 %reduce-scatter.12.cloned.1.call-start = ((), (), s32[]{:S(2)}) async-start(), calls=%async_computation.8 | async-start | bytes 10027008
  272.0 68.6 %copy-start.1 = (f32[384,768]{1,0:T(8,128)S(1)}, f32[384,768]{1,0:T(8,128)}, u32[]{:S(2)}) copy-start(f32[384,768]{1,0:T(8,128)} %param.16) | copy-start | bytes 3538948
  272.0 317.1 %all-gather.8.cloned.1.call-start = ((), (), s32[]{:S(2)}) async-start(), calls=%async_computation.5 | async-start | bytes 10027008 | tf_op jit(solution)/shard_map/all_gather | solution.py:70
Sparse Core Ops, SparseCore 0:
  9.7 103.3 all-gather.3
  136.8 106.7 reduce-scatter.9
  246.3 82.4 all-gather.5
  333.7 62.7 reduce-scatter.7
  401.2 107.2 reduce-scatter.11
  511.5 77.5 all-gather.7
where the time goes:
time: 605 us; the launch traced here: 604 us
  waiting for transfers between devices  511 us (84%)
  local copies, waits for them, and re-layouts  38.7 us (6%)
  matrix products  35.4 us (6%)
  between operations  14.2 us (2%)
    unnamed x8, waiting for transfers between devices  218 us
    all_gather x1, waiting for transfers between devices, shards(): rows_basis = lax.all_gather(basis_in, 'owner', axis=0, tiled=True)  105 us
    all_gather x1, waiting for transfers between devices, shards(): precond = lax.all_gather(local_update, 'dp', axis=0, tiled=True)  75.8 us
    all_gather x1, waiting for transfers between devices, shards(): lax.all_gather(scaled, 'dp', axis=0, tiled=True)  56.7 us
    reduce_scatter x1, waiting for transfers between devices, shards(): lax.psum_scatter(lax.dot_general(grad_columns, grad_columns, (((0,), (0,)...  55.5 us
    unnamed x15, local copies, waits for them, and re-layouts  38.7 us
  transfers between devices with their start and end apart: 6, of which 6 were waited for; matrix products, arithmetic and copies ran while one was open for 7% of the time, Pallas kernels for 0%

commit v1 on v0

v1 whole, which is shorter than its diff:
```python
import functools

import jax
import jax.numpy as jnp
from jax import lax
from jax.experimental import pallas as pl
from jax.experimental.pallas import tpu as pltpu
from jax.sharding import PartitionSpec as P

damping = 0.3
factor_decay = 0.9
MESH = pl.DeviceIdType.MESH
CHUNKS = 2
MESSAGES = 160
F32 = jnp.float32
BF16 = jnp.bfloat16


def dot_rows(left, right):
    return lax.dot_general(left, right, (((0,), (0,)), ((), ())), preferred_element_type=F32)


def dot(left, right):
    return jnp.dot(left, right, preferred_element_type=F32)


class Message:
    def __init__(self, pool, source, target, to):
        number = pool[2]
        pool[2] += 1
        self.copy = pltpu.make_async_remote_copy(
            src_ref=source,
            dst_ref=target,
            send_sem=pool[0].at[number],
            recv_sem=pool[1].at[number],
            device_id=to,
            device_id_type=MESH,
        )

    def start(self):
        self.copy.start()
        return self

    def arrived(self):
        self.copy.wait_recv()

    def sent(self):
        self.copy.wait_send()


class Gather:
    def __init__(self, pool, region, place, plus, minus):
        self.region, self.place, self.plus, self.minus, self.pool = region, place, plus, minus, pool
        self.own = {}
        self.passed = []

    def message(self, shard, half, to):
        piece = self.region(shard, half)
        return Message(self.pool, piece, piece, to).start()

    def start(self, half):
        order = (("plus", self.plus), ("minus", self.minus))
        for name, to in order if half == 0 else order[::-1]:
            self.own[name, half] = self.message(self.place, half, to)

    def forward(self):
        below, above = lax.rem(self.place + 3, 4), lax.rem(self.place + 1, 4)
        self.own["plus", 0].arrived()
        self.passed.append(self.message(below, 0, self.plus))
        self.own["minus", 1].arrived()
        self.passed.append(self.message(above, 1, self.minus))

    def near(self):
        self.own["minus", 0].arrived()
        self.own["plus", 1].arrived()

    def far(self):
        for message in self.passed:
            message.arrived()

    def sent(self):
        for message in list(self.own.values()) + self.passed:
            message.sent()


class Scatter:
    def __init__(self, pool, mine, transit, slots, place, plus, minus):
        self.pool, self.mine, self.transit, self.slots = pool, mine, transit, slots
        self.plus, self.minus = plus, minus
        self.here = place
        self.above, self.below, self.far = (lax.rem(place + step, 4) for step in (1, 3, 2))
        self.messages = []

    def send(self, source, target, to):
        message = Message(self.pool, source, target, to).start()
        self.messages.append(message)
        return message

    def start_far(self):
        self.up = self.send(self.mine(self.far, 0), self.transit(0), self.plus)
        self.down = self.send(self.mine(self.far, 1), self.transit(1), self.minus)

    def start_near(self):
        self.direct_up = self.send(self.mine(self.above, 1), self.slots(0), self.plus)
        self.direct_down = self.send(self.mine(self.below, 0), self.slots(1), self.minus)

    def forward(self):
        self.up.arrived()
        piece = self.mine(self.above, 0)
        piece[...] = (piece[...].astype(F32) + self.transit(0)[...].astype(F32)).astype(BF16)
        self.sum_up = self.send(piece, self.slots(2), self.plus)
        self.down.arrived()
        piece = self.mine(self.below, 1)
        piece[...] = (piece[...].astype(F32) + self.transit(1)[...].astype(F32)).astype(BF16)
        self.sum_down = self.send(piece, self.slots(3), self.minus)

    def arrived(self, half):
        if half == 0:
            self.direct_down.arrived()
            self.sum_up.arrived()
        else:
            self.direct_up.arrived()
            self.sum_down.arrived()

    def total(self, half):
        one, two = (1, 2) if half == 0 else (0, 3)
        return (
            self.mine(self.here, half)[...].astype(F32)
            + self.slots(one)[...].astype(F32)
            + self.slots(two)[...].astype(F32)
        )

    def sent(self):
        for message in self.messages:
            message.sent()


def kernel(
    inputs,
    grads,
    kernel_grad,
    basis_in,
    basis_out,
    eigen_in,
    eigen_out,
    gathered,
    in_cov,
    out_cov,
    basis,
    turned,
    part,
    part_transit,
    part_slots,
    scaled,
    eigen_rows,
    eigen_columns,
    away,
    away_in,
    home,
    home_sum,
    home_transit,
    home_slots,
    tokens,
    token_columns,
    grad_columns,
    grad_part,
    cov,
    cov_transit,
    cov_slots,
    cov_across,
    grad_tile,
    basis_out_tile,
    local,
    send,
    receive,
):
    pool = [send, receive, 0]
    rows = kernel_grad.shape[0]
    width = kernel_grad.shape[1]
    strip = basis_in.shape[0]
    out_rows = out_cov.shape[0]
    narrow = width // 4
    dp, owner = lax.axis_index("dp"), lax.axis_index("owner")
    xh, z, c = dp // 8, lax.rem(dp // 2, 4), lax.rem(dp, 2)
    y, xl = owner // 2, lax.rem(owner, 2)
    x = xh * 2 + xl

    def device(x, y, z, c):
        x, y, z, c = lax.rem(x, 4), lax.rem(y, 4), lax.rem(z, 4), lax.rem(c, 2)
        return (x // 2) * 8 + z * 2 + c, y * 2 + lax.rem(x, 2)

    x_up, x_down, x_far = device(x + 1, y, z, c), device(x + 3, y, z, c), device(x + 2, y, z, c)
    y_up, y_down = device(x, y + 1, z, c), device(x, y + 3, z, c)
    z_up, z_down, z_far = device(x, y, z + 1, c), device(x, y, z + 3, c), device(x, y, z + 2, c)
    core = device(x, y, z, c + 1)
    x_pair = device(xh * 2 + 1 - xl, y, z, c)
    plane = [(step, side) for step in (2, 1, 3, 0) for side in (0, 1) if (step, side) != (0, 0)]

    locals_started = []

    def fetch(source, target):
        copy = pltpu.make_async_copy(source, target, local.at[len(locals_started)])
        copy.start()
        locals_started.append(copy)
        return copy

    def block_columns(ref, block):
        return ref.at[:, pl.ds(pl.multiple_of(block * rows, rows), rows)]

    def owner_columns(ref):
        return ref.at[:, pl.ds(pl.multiple_of(owner * width, width), width)]

    got_grad = fetch(kernel_grad, grad_tile)
    got_basis_out = fetch(basis_out, basis_out_tile)

    barrier = pltpu.get_barrier_semaphore()
    partners = [device(x + step, y, z, c + side) for step, side in plane]
    partners += [y_up, y_down, z_up, z_down, z_far]
    for partner in partners:
        pl.semaphore_signal(barrier, inc=1, device_id=partner, device_id_type=MESH)

    def strip_rows(x, y, c):
        block = (x // 2) * 2 + c
        start = pl.multiple_of((y * 2 + lax.rem(x, 2)) * strip, strip)
        return block, pl.ds(start, strip)

    my_block, my_rows = strip_rows(x, y, c)

    def basis_piece(t):
        return basis.at[my_block, my_rows, t * rows : (t + 1) * rows]

    own_basis = [
        fetch(block_columns(basis_in, xh * 8 + (2 * xl + t) * 2 + c), basis_piece(t)) for t in range(2)
    ]
    far, above, below = lax.rem(z + 2, 4), lax.rem(z + 1, 4), lax.rem(z + 3, 4)
    order = [far, above, below, z]
    got_tokens = {}
    got_columns = fetch(owner_columns(inputs), token_columns.at[0])
    got_grad_columns = fetch(owner_columns(grads), grad_columns.at[0])
    for step in range(4):
        for high in range(2):
            got_tokens[step, high] = fetch(
                block_columns(inputs, high * 8 + order[step] * 2 + c), tokens.at[0, step * 2 + high]
            )

    pl.semaphore_wait(barrier, len(partners))

    scatter_basis = []
    for step, side in plane:
        to_x = lax.rem(x + step, 4)
        to_c = lax.rem(c + side, 2)
        for t in range(2):
            block = (to_x // 2) * 8 + (2 * lax.rem(to_x, 2) + t) * 2 + to_c
            scatter_basis.append(
                Message(
                    pool,
                    block_columns(basis_in, block),
                    basis_piece(t),
                    device(x + step, y, z, c + side),
                ).start()
            )
    small = []
    for to in (z_up, z_down, z_far):
        small.append(Message(pool, eigen_in, eigen_rows.at[z], to).start())
    small.append(Message(pool, eigen_out, eigen_columns.at[xl], x_pair).start())

    token_messages = {}
    column_message = Message(pool, owner_columns(inputs), token_columns.at[1], core).start()
    for step in range(4):
        for high in range(2):
            token_messages[step, high] = Message(
                pool,
                block_columns(inputs, high * 8 + order[step] * 2 + 1 - c),
                tokens.at[1, step * 2 + high],
                core,
            ).start()
    grad_message = Message(pool, owner_columns(grads), grad_columns.at[1], core).start()

    got_grad.wait()
    got_basis_out.wait()

    def turned_tile(x, c):
        return turned.at[lax.rem(x, 2), (x // 2) * 2 + c]

    turned_tile(x, c)[...] = dot(grad_tile[...], basis_out_tile[...]).astype(BF16)
    half_rows = rows // 2

    def turned_region(place, half):
        return turned.at[lax.rem(place, 2), (place // 2) * 2 + c, half * half_rows : (half + 1) * half_rows]

    turned_gather = Gather(pool, turned_region, x, x_up, x_down)
    turned_gather.start(0)
    turned_gather.start(1)

    def to_core(step):
        tile = turned_tile(lax.rem(x + step, 4), c)
        return Message(pool, tile, tile, core).start()

    turned_core = [to_core(0)]

    for copy in own_basis:
        copy.wait()
    for message in scatter_basis:
        message.arrived()

    def basis_region(place, half):
        start = pl.multiple_of(place * 2 * strip, 2 * strip)
        return basis.at[half * 2 : half * 2 + 2, pl.ds(start, 2 * strip), :]

    basis_gather = Gather(pool, basis_region, y, y_up, y_down)
    basis_gather.start(0)
    basis_gather.start(1)

    def cov_mine(place, half):
        return cov.at[half, place]

    cov_scatter = Scatter(
        pool, cov_mine, lambda half: cov_transit.at[half], lambda slot: cov_slots.at[slot], z, z_up, z_down
    )
    got_columns.wait()
    got_grad_columns.wait()
    column_message.arrived()
    grad_message.arrived()
    grad_part[...] = (
        dot_rows(grad_columns[0], grad_columns[0]) + dot_rows(grad_columns[1], grad_columns[1])
    ).astype(BF16)

    def cov_product(step):
        for high in range(2):
            got_tokens[step, high].wait()
            token_messages[step, high].arrived()
        place = order[step]

        def product(high, unused):
            tile = dot_rows(tokens[0, step * 2 + high], token_columns[0])
            tile = tile + dot_rows(tokens[1, step * 2 + high], token_columns[1])
            cov[high, place, :rows] = tile.astype(BF16)
            start = pl.multiple_of((high * 8 + place * 2 + c) * out_rows, out_rows)
            cov[high, place, rows:] = grad_part[pl.ds(start, out_rows), :]
            return unused

        lax.fori_loop(0, 2, product, 0)

    cov_product(0)
    cov_scatter.start_far()
    turned_gather.forward()
    turned_gather.near()
    turned_core += [to_core(1), to_core(3)]
    basis_gather.forward()
    cov_product(1)
    cov_product(2)
    cov_scatter.start_near()
    cov_product(3)
    turned_gather.far()
    turned_core.append(to_core(2))
    basis_gather.near()
    basis_gather.far()
    for message in turned_core:
        message.arrived()

    def part_mine(place, half):
        return part.at[half, pl.ds(pl.multiple_of(place * narrow, narrow), narrow), :]

    part_scatter = Scatter(
        pool, part_mine, lambda half: part_transit.at[half], lambda slot: part_slots.at[slot], z, z_up, z_down
    )

    def rotate(t):
        start = pl.multiple_of(t * rows, rows)
        left = basis[:, :, pl.ds(start, rows)].reshape(4 * rows, rows)

        def one(side, unused):
            right = turned[side].reshape(4 * rows, width)
            part[side, pl.ds(start, rows), :] = dot_rows(left, right).astype(BF16)
            return unused

        lax.fori_loop(0, 2, one, 0)

    rotate(1 - z // 2)
    part_scatter.start_far()
    rotate(z // 2)
    part_scatter.start_near()

    for message in small:
        message.arrived()
    eigen_rows[z] = eigen_in[...]
    eigen_columns[xl] = eigen_out[...]
    line = eigen_rows[2 * xl + z // 2]
    line = jnp.where(lax.rem(z, 2) == 0, line[:, :narrow], line[:, narrow:])
    column = jnp.transpose(jnp.broadcast_to(line[:1], (128, narrow)))[:, :1]

    part_scatter.forward()

    def scaled_region(place, half):
        return scaled.at[half, pl.ds(pl.multiple_of(place * narrow, narrow), narrow), :]

    scaled_gather = Gather(pool, scaled_region, z, z_up, z_down)
    for half in range(2):
        part_scatter.arrived(half)
        divisor = column * eigen_columns[half][:1] + damping
        scaled_region(z, half)[...] = (part_scatter.total(half) / divisor).astype(BF16)
        scaled_gather.start(half)
    scaled_gather.forward()
    cov_scatter.forward()
    scaled_gather.near()
    scaled_gather.far()

    lines = rows // CHUNKS
    half_width = width // 2
    half_lines = lines // 2
    finishing = []
    scatters = []
    for chunk in range(CHUNKS):
        chunk_rows = slice(chunk * lines, (chunk + 1) * lines)

        def partial(side, target):
            def one(place, unused):
                left = basis[(place // 2) * 2 + side, chunk_rows, :]
                target[place] = dot(left, scaled[lax.rem(place, 2)]).astype(target.dtype)
                return unused

            lax.fori_loop(0, 4, one, 0)

        partial(1 - c, away.at[chunk])
        crossing = Message(pool, away.at[chunk], away_in.at[chunk], core).start()
        finishing.append(crossing)
        partial(c, home)
        crossing.arrived()
        home_sum[chunk] = (home[...] + away_in[chunk].astype(F32)).astype(BF16)

        def home_mine(place, half, chunk=chunk):
            return home_sum.at[chunk, place, :, half * half_width : (half + 1) * half_width]

        scatter = Scatter(
            pool,
            home_mine,
            lambda half, chunk=chunk: home_transit.at[chunk, half],
            lambda slot, chunk=chunk: home_slots.at[chunk, slot],
            x,
            x_up,
            x_down,
        )
        scatter.start_far()
        scatter.start_near()
        scatters.append(scatter)

    ends = []
    for chunk in range(CHUNKS):
        scatter = scatters[chunk]
        scatter.forward()
        scatter.arrived(0)
        scatter.arrived(1)
        restored = jnp.concatenate([scatter.total(0), scatter.total(1)], axis=1).astype(BF16)
        new = lax.dot_general(restored, basis_out_tile[...], (((1,), (1,)), ((), ())), preferred_element_type=F32)

        def region(place, half, high, chunk=chunk):
            start = (high * 8 + place * 2 + c) * rows + chunk * lines
            if half is None:
                return gathered.at[pl.ds(pl.multiple_of(start, 16), lines), :]
            return gathered.at[pl.ds(pl.multiple_of(start + half * half_lines, 16), half_lines), :]

        own_gather = Gather(pool, functools.partial(region, high=xh), z, z_up, z_down)
        other_gather = Gather(pool, functools.partial(region, high=1 - xh), z, z_up, z_down)
        mine = region(z, None, xh)
        mine[...] = new.astype(BF16)
        own_gather.start(0)
        own_gather.start(1)
        across = Message(pool, mine, mine, x_far).start()
        finishing += [across, Message(pool, mine, mine, core).start()]
        ends.append((own_gather, other_gather, across, region))

    cov_scatter.arrived(0)
    cov_scatter.arrived(1)
    totals = [cov_scatter.total(0), cov_scatter.total(1)]
    cov[1 - xh, z] = jnp.where(xh == 0, totals[1], totals[0]).astype(BF16)
    cov_message = Message(pool, cov.at[1 - xh, z], cov_across, x_far).start()

    to_core_last = []
    for own_gather, other_gather, across, region in ends:
        across.arrived()
        other_gather.start(0)
        other_gather.start(1)
        received = region(z, None, 1 - xh)
        to_core_last.append(Message(pool, received, received, core).start())
    for own_gather, other_gather, across, region in ends:
        for gather, high in ((own_gather, xh), (other_gather, 1 - xh)):
            gather.forward()
            gather.near()
            for place in (above, below):
                received = region(place, None, high)
                to_core_last.append(Message(pool, received, received, core).start())

    cov_message.arrived()
    total = jnp.where(xh == 0, totals[0], totals[1]) + cov_across[...].astype(F32)
    in_cov[...] = total[:rows]
    out_cov[...] = total[rows:]

    for own_gather, other_gather, across, region in ends:
        for gather, high in ((own_gather, xh), (other_gather, 1 - xh)):
            gather.far()
            received = region(far, None, high)
            to_core_last.append(Message(pool, received, received, core).start())

    for message in to_core_last:
        message.arrived()
    for own_gather, other_gather, across, region in ends:
        own_gather.sent()
        other_gather.sent()
    for chunk, message in enumerate(finishing[CHUNKS:]):
        if chunk % 2 == 1:
            message.arrived()
    for message in finishing + to_core_last + scatter_basis + small + turned_core:
        message.sent()
    for message in list(token_messages.values()) + [column_message, grad_message, cov_message]:
        message.sent()
    for group in [turned_gather, basis_gather, scaled_gather, cov_scatter, part_scatter] + scatters:
        group.sent()


def finish(gathered, in_cov, out_cov, old_in, old_out, precond, in_factor, out_factor, sem, tokens):
    copy = pltpu.make_async_copy(gathered, precond, sem)
    copy.start()
    in_factor[...] = factor_decay * old_in[...] + (1.0 - factor_decay) * in_cov[...] / tokens
    out_factor[...] = factor_decay * old_out[...] + (1.0 - factor_decay) * out_cov[...] / tokens
    copy.wait()


def shards(
    inputs, out_grads, kernel_grad, basis_in, basis_out, eigen_in, eigen_out, old_in_factor, old_out_factor
):
    rows, width = kernel_grad.shape
    strip = basis_in.shape[0]
    tokens = inputs.shape[0]
    out_rows = old_out_factor.shape[0]
    deep = rows + out_rows
    total = 16 * rows
    lines = rows // CHUNKS
    narrow = width // 4
    anywhere = pl.BlockSpec(memory_space=pl.ANY)
    vmem = pl.BlockSpec(memory_space=pltpu.VMEM)
    scratch = [
        pltpu.VMEM((4, rows, 2 * rows), BF16),
        pltpu.VMEM((2, 4, rows, width), BF16),
        pltpu.VMEM((2, 4 * narrow, width), BF16),
        pltpu.VMEM((2, narrow, width), BF16),
        pltpu.VMEM((4, narrow, width), BF16),
        pltpu.VMEM((2, 4 * narrow, width), BF16),
        pltpu.VMEM((4, 8, rows), F32),
        pltpu.VMEM((2, 8, width), F32),
        pltpu.VMEM((CHUNKS, 4, lines, width), BF16),
        pltpu.VMEM((CHUNKS, 4, lines, width), BF16),
        pltpu.VMEM((4, lines, width), F32),
        pltpu.VMEM((CHUNKS, 4, lines, width), BF16),
        pltpu.VMEM((CHUNKS, 2, lines, width // 2), BF16),
        pltpu.VMEM((CHUNKS, 4, lines, width // 2), BF16),
        pltpu.VMEM((2, 8, tokens, rows), BF16),
        pltpu.VMEM((2, tokens, width), BF16),
        pltpu.VMEM((2, tokens, width), BF16),
        pltpu.VMEM((width, width), BF16),
        pltpu.VMEM((2, 4, deep, width), BF16),
        pltpu.VMEM((2, deep, width), BF16),
        pltpu.VMEM((4, deep, width), BF16),
        pltpu.VMEM((deep, width), BF16),
        pltpu.VMEM((rows, width), BF16),
        pltpu.VMEM((width, width), BF16),
        pltpu.SemaphoreType.DMA((16,)),
        pltpu.SemaphoreType.DMA((MESSAGES,)),
        pltpu.SemaphoreType.DMA((MESSAGES,)),
    ]
    gathered, in_cov, out_cov = pl.pallas_call(
        kernel,
        out_shape=(
            pltpu.VMEM((total, width), BF16),
            jax.ShapeDtypeStruct((rows, width), F32),
            jax.ShapeDtypeStruct((out_rows, width), F32),
        ),
        in_specs=[anywhere] * 5 + [vmem] * 2,
        out_specs=(vmem, vmem, vmem),
        scratch_shapes=scratch,
        compiler_params=pltpu.CompilerParams(
            collective_id=0, has_side_effects=True, vmem_limit_bytes=52 * 2**20
        ),
        cost_estimate=pl.CostEstimate(flops=2 * 10**10, bytes_accessed=4 * 10**7, transcendentals=0),
        name="precondition",
    )(
        inputs,
        out_grads,
        kernel_grad,
        basis_in,
        basis_out,
        jnp.broadcast_to(eigen_in[None, :], (8, rows)),
        jnp.broadcast_to(eigen_out[None, :], (8, width)),
    )
    return pl.pallas_call(
        functools.partial(finish, tokens=16 * tokens),
        out_shape=(
            jax.ShapeDtypeStruct((total, width), BF16),
            jax.ShapeDtypeStruct((rows, width), F32),
            jax.ShapeDtypeStruct((out_rows, width), F32),
        ),
        in_specs=[vmem] * 5,
        out_specs=(anywhere, vmem, vmem),
        scratch_shapes=[pltpu.SemaphoreType.DMA],
        compiler_params=pltpu.CompilerParams(vmem_limit_bytes=40 * 2**20),
        name="finish",
    )(gathered, in_cov, out_cov, old_in_factor, old_out_factor)


def solution(mesh):
    in_specs = (
        P("dp", None),
        P("dp", None),
        P("dp", "owner"),
        P(("dp", "owner"), None),
        P("owner", None),
        P("dp"),
        P("owner"),
        P("dp", "owner"),
        P(("owner", "dp"), None),
    )
    out_specs = (P(None, "owner"), P("dp", "owner"), P(("owner", "dp"), None))
    return jax.shard_map(shards, mesh=mesh, in_specs=in_specs, out_specs=out_specs, check_vma=False)
```

time: 605 us -> 178 us (0.29)
  waiting for transfers between devices: 511 us -> 0 us
  Pallas kernels: 0 us -> 173 us
  matrix products: 35.4 us -> 0 us
  local copies, waits for them, and re-layouts: 38.7 us -> 4.76 us
  between operations: 14.2 us -> 0.67 us
    all_gather x3 -> x0, waiting for transfers between devices: 238 us -> none  [the longest x1 105 us: shards(): rows_basis = lax.all_gather(basis_in, 'owner', axis=0, tiled=True)]
    unnamed x8 -> x0, waiting for transfers between devices: 218 us -> none
    pallas_call x0 -> x2, Pallas kernels: none -> 173 us  [the longest x1 168 us: shards(): pl.pallas_call(kernel, out_shape=(pltpu.VMEM((total, width), BF16), jax.S...]
    reduce_scatter x1 -> x0, waiting for transfers between devices: 55.5 us -> none  [shards(): lax.psum_scatter(lax.dot_general(grad_columns, grad_columns, (((0,), (0,)...]
    unnamed x15 -> x8, local copies, waits for them, and re-layouts: 38.7 us -> 2.18 us
    dot_general x4 -> x0, matrix products: 35.4 us -> none  [the longest x1 11.7 us: shards(): lax.dot_general(restored, basis_out, (((1,), (1,)), ((), ())), preferred_...]
  transfers between devices with their start and end apart: 6 -> 0, of which waited for: 6 -> 0; matrix products, arithmetic and copies ran while one was open for 7% -> 0% of each run, Pallas kernels for 0% -> 0%
where the time goes in v1:
time: 178 us
  Pallas kernels  173 us (97%)
  local copies, waits for them, and re-layouts  4.76 us (3%)
    pallas_call x1, Pallas kernels, shards(): pl.pallas_call(kernel, out_shape=(pltpu.VMEM((total, width), BF16), jax.S...  168 us
    pallas_call x1, Pallas kernels, shards(): pl.pallas_call(functools.partial(finish, tokens=16 * tokens), out_shape=(...  4.8 us

profile of v1, /device:TPU:1, one launch (start us, length us, event | category | flops | bytes accessed | tf_op | source)
XLA Modules:
  0.0 178.1 jit_solution(17326961606707380295)
XLA Ops:
  0.6 1.3 broadcast_in_dim.4.eigen_in
  1.9 1.3 broadcast_in_dim.5.eigen_out
  3.2 0.0 copy-start
  3.2 0.0 copy-start.2
  3.2 167.9 %precondition.1 = (bf16[6144,768]{1,0:T(8,128)(2,1)S(1)}, f32[384,768]{1,0:T(8,128)}, f32[48,768]{1,0:T(8,128)}) custom-call(bf16[512,6144]{1,0:T(8,128)(2,1)} %inputs.1, bf16[512,6144]{1,0:T(8,128)(2,1)} %grads.1, bf16[384,768]{1,0:T(8,128)(2,1)} %kernel_grad.1, bf16[48,6144]{1,0:T(8,128)(2,1)} %basis_in.1, bf16[768,768]{1,0:T(8,128)(2,1)} %basis_out.1, ...), custom_call_target="tpu_custom_call" | custom-call | flops 20000000000 | bytes 40000000 | tf_op jit(solution)/shard_map/precondition/pallas_call | solution.py:570
  171.1 0.0 copy-done
  171.1 0.0 copy-done.2
  171.1 0.0 copy-start.1
  171.1 1.3 copy-done.1
  172.4 0.0 copy-start.3
  172.4 0.9 copy-done.3
  173.3 4.8 %finish.1 = (bf16[6144,768]{1,0:T(8,128)(2,1)}, f32[384,768]{1,0:T(8,128)}, f32[48,768]{1,0:T(8,128)}) custom-call(bf16[6144,768]{1,0:T(8,128)(2,1)S(1)} %get-tuple-element.6.gathered, f32[384,768]{1,0:T(8,128)S(1)} %copy-done.1, f32[48,768]{1,0:T(8,128)S(1)} %copy-done.3, f32[384,768]{1,0:T(8,128)S(1)} %copy-done, f32[48,768]{1,0:T(8,128)S(1)} %copy-done.2), custom_call_target="tpu_custom_call" | custom-call | tf_op jit(solution)/shard_map/finish/pallas_call | solution.py:594
Async XLA Ops:
  3.2 167.9 %copy-start = (f32[384,768]{1,0:T(8,128)S(1)}, f32[384,768]{1,0:T(8,128)}, u32[]{:S(2)}) copy-start(f32[384,768]{1,0:T(8,128)} %old_in.1) | copy-start | bytes 3538948
  3.2 167.9 %copy-start.2 = (f32[48,768]{1,0:T(8,128)S(1)}, f32[48,768]{1,0:T(8,128)}, u32[]{:S(2)}) copy-start(f32[48,768]{1,0:T(8,128)} %old_out.1) | copy-start | bytes 442372
  171.1 1.3 copy-start.1
  172.4 0.9 copy-start.3

commit v2 on v1

--- a/solution.py
+++ b/solution.py
@@ -10,8 +10,9 @@
 damping = 0.3
 factor_decay = 0.9
 MESH = pl.DeviceIdType.MESH
-CHUNKS = 2
-MESSAGES = 160
+CHUNKS = 3
+WAVES = 2
+MESSAGES = 256
 F32 = jnp.float32
 BF16 = jnp.bfloat16
 
@@ -104,15 +105,20 @@
         self.direct_up = self.send(self.mine(self.above, 1), self.slots(0), self.plus)
         self.direct_down = self.send(self.mine(self.below, 0), self.slots(1), self.minus)
 
-    def forward(self):
-        self.up.arrived()
-        piece = self.mine(self.above, 0)
-        piece[...] = (piece[...].astype(F32) + self.transit(0)[...].astype(F32)).astype(BF16)
-        self.sum_up = self.send(piece, self.slots(2), self.plus)
-        self.down.arrived()
-        piece = self.mine(self.below, 1)
-        piece[...] = (piece[...].astype(F32) + self.transit(1)[...].astype(F32)).astype(BF16)
-        self.sum_down = self.send(piece, self.slots(3), self.minus)
+    def add(self):
+        for message, half, place in ((self.up, 0, self.above), (self.down, 1, self.below)):
+            message.arrived()
+            piece = self.mine(place, half)
+            piece[...] = (piece[...].astype(F32) + self.transit(half)[...].astype(F32)).astype(BF16)
+            if half == 0:
+                self.pass_up()
+        self.pass_down()
+
+    def pass_up(self):
+        self.sum_up = self.send(self.mine(self.above, 0), self.slots(2), self.plus)
+
+    def pass_down(self):
+        self.sum_down = self.send(self.mine(self.below, 1), self.slots(3), self.minus)
 
     def arrived(self, half):
         if half == 0:
@@ -123,11 +129,10 @@
             self.sum_down.arrived()
 
     def total(self, half):
-        one, two = (1, 2) if half == 0 else (0, 3)
         return (
             self.mine(self.here, half)[...].astype(F32)
-            + self.slots(one)[...].astype(F32)
-            + self.slots(two)[...].astype(F32)
+            + self.slots(1 - half)[...].astype(F32)
+            + self.slots(2 + half)[...].astype(F32)
         )
 
     def sent(self):
@@ -158,6 +163,7 @@
     away_in,
     home,
     home_sum,
+    restored_part,
     home_transit,
     home_slots,
     tokens,
@@ -193,8 +199,10 @@
     y_up, y_down = device(x, y + 1, z, c), device(x, y + 3, z, c)
     z_up, z_down, z_far = device(x, y, z + 1, c), device(x, y, z + 3, c), device(x, y, z + 2, c)
     core = device(x, y, z, c + 1)
-    x_pair = device(xh * 2 + 1 - xl, y, z, c)
-    plane = [(step, side) for step in (2, 1, 3, 0) for side in (0, 1) if (step, side) != (0, 0)]
+    pair = xh * 2 + 1 - xl
+    cross = lax.rem(x + 2 * xl + 3, 4)
+    plane = [(step, side) for step in (-1, 0, -2, 2) for side in (0, 1) if (step, side) != (0, 0)]
+    x_pair = device(pair, y, z, c)
 
     locals_started = []
 
@@ -214,7 +222,7 @@
     got_basis_out = fetch(basis_out, basis_out_tile)
 
     barrier = pltpu.get_barrier_semaphore()
-    partners = [device(x + step, y, z, c + side) for step, side in plane]
+    partners = [device(x + step, y, z, c + side) for step in range(4) for side in range(2) if step + side > 0]
     partners += [y_up, y_down, z_up, z_down, z_far]
     for partner in partners:
         pl.semaphore_signal(barrier, inc=1, device_id=partner, device_id_type=MESH)
@@ -245,24 +253,21 @@
 
     pl.semaphore_wait(barrier, len(partners))
 
-    scatter_basis = []
+    scatter_basis = {}
     for step, side in plane:
-        to_x = lax.rem(x + step, 4)
+        to = {-1: pair, -2: cross, 0: x, 2: lax.rem(x + 2, 4)}[step]
         to_c = lax.rem(c + side, 2)
         for t in range(2):
-            block = (to_x // 2) * 8 + (2 * lax.rem(to_x, 2) + t) * 2 + to_c
-            scatter_basis.append(
-                Message(
-                    pool,
-                    block_columns(basis_in, block),
-                    basis_piece(t),
-                    device(x + step, y, z, c + side),
-                ).start()
-            )
+            block = (to // 2) * 8 + (2 * lax.rem(to, 2) + t) * 2 + to_c
+            scatter_basis[step, side, t] = Message(
+                pool, block_columns(basis_in, block), basis_piece(t), device(to, y, z, to_c)
+            ).start()
     small = []
+    eigen_rows[z] = jnp.broadcast_to(eigen_in[...].reshape(1, rows), (8, rows))
+    eigen_columns[xl] = jnp.broadcast_to(eigen_out[...].reshape(1, width), (8, width))
     for to in (z_up, z_down, z_far):
-        small.append(Message(pool, eigen_in, eigen_rows.at[z], to).start())
-    small.append(Message(pool, eigen_out, eigen_columns.at[xl], x_pair).start())
+        small.append(Message(pool, eigen_rows.at[z], eigen_rows.at[z], to).start())
+    small.append(Message(pool, eigen_columns.at[xl], eigen_columns.at[xl], x_pair).start())
 
     token_messages = {}
     column_message = Message(pool, owner_columns(inputs), token_columns.at[1], core).start()
@@ -288,28 +293,31 @@
     def turned_region(place, half):
         return turned.at[lax.rem(place, 2), (place // 2) * 2 + c, half * half_rows : (half + 1) * half_rows]
 
-    turned_gather = Gather(pool, turned_region, x, x_up, x_down)
-    turned_gather.start(0)
-    turned_gather.start(1)
-
     def to_core(step):
         tile = turned_tile(lax.rem(x + step, 4), c)
         return Message(pool, tile, tile, core).start()
 
-    turned_core = [to_core(0)]
-
+    turned_gather = Gather(pool, turned_region, x, x_up, x_down)
+
+    def basis_region(place, half):
+        start = pl.multiple_of(place * 2 * strip, 2 * strip)
+        high = 2 * lax.rem(xh + half, 2)
+        return basis.at[pl.ds(high, 2), pl.ds(start, 2 * strip), :]
+
+    basis_gather = Gather(pool, basis_region, y, y_up, y_down)
     for copy in own_basis:
         copy.wait()
-    for message in scatter_basis:
-        message.arrived()
-
-    def basis_region(place, half):
-        start = pl.multiple_of(place * 2 * strip, 2 * strip)
-        return basis.at[half * 2 : half * 2 + 2, pl.ds(start, 2 * strip), :]
-
-    basis_gather = Gather(pool, basis_region, y, y_up, y_down)
+    for (step, side, t), message in scatter_basis.items():
+        if step in (-1, 0):
+            message.arrived()
     basis_gather.start(0)
+    turned_gather.start(0)
+    for (step, side, t), message in scatter_basis.items():
+        if step not in (-1, 0):
+            message.arrived()
     basis_gather.start(1)
+    turned_gather.start(1)
+    turned_core = [to_core(0)]
 
     def cov_mine(place, half):
         return cov.at[half, place]
@@ -358,171 +366,239 @@
     for message in turned_core:
         message.arrived()
 
-    def part_mine(place, half):
-        return part.at[half, pl.ds(pl.multiple_of(place * narrow, narrow), narrow), :]
-
-    part_scatter = Scatter(
-        pool, part_mine, lambda half: part_transit.at[half], lambda slot: part_slots.at[slot], z, z_up, z_down
-    )
-
-    def rotate(t):
+    wave = width // WAVES
+
+    def rows_of(ref, place, half, number):
+        start = pl.multiple_of(place * narrow, narrow)
+        return ref.at[half, pl.ds(start, narrow), number * wave : (number + 1) * wave]
+
+    part_scatters = [
+        Scatter(
+            pool,
+            lambda place, half, number=number: rows_of(part, place, half, number),
+            lambda half, number=number: part_transit.at[number, half],
+            lambda slot, number=number: part_slots.at[number, slot],
+            z,
+            z_up,
+            z_down,
+        )
+        for number in range(WAVES)
+    ]
+
+    def rotate(t, number):
         start = pl.multiple_of(t * rows, rows)
         left = basis[:, :, pl.ds(start, rows)].reshape(4 * rows, rows)
 
         def one(side, unused):
-            right = turned[side].reshape(4 * rows, width)
-            part[side, pl.ds(start, rows), :] = dot_rows(left, right).astype(BF16)
+            right = turned[side, :, :, number * wave : (number + 1) * wave].reshape(4 * rows, wave)
+            part[side, pl.ds(start, rows), number * wave : (number + 1) * wave] = dot_rows(left, right).astype(BF16)
             return unused
 
         lax.fori_loop(0, 2, one, 0)
 
-    rotate(1 - z // 2)
-    part_scatter.start_far()
-    rotate(z // 2)
-    part_scatter.start_near()
+    for number, scatter in enumerate(part_scatters):
+        rotate(1 - z // 2, number)
+        scatter.start_far()
+        if number > 0:
+            part_scatters[number - 1].add()
+        rotate(z // 2, number)
+        scatter.start_near()
 
     for message in small:
         message.arrived()
-    eigen_rows[z] = eigen_in[...]
-    eigen_columns[xl] = eigen_out[...]
     line = eigen_rows[2 * xl + z // 2]
     line = jnp.where(lax.rem(z, 2) == 0, line[:, :narrow], line[:, narrow:])
     column = jnp.transpose(jnp.broadcast_to(line[:1], (128, narrow)))[:, :1]
 
-    part_scatter.forward()
-
-    def scaled_region(place, half):
-        return scaled.at[half, pl.ds(pl.multiple_of(place * narrow, narrow), narrow), :]
-
-    scaled_gather = Gather(pool, scaled_region, z, z_up, z_down)
-    for half in range(2):
-        part_scatter.arrived(half)
-        divisor = column * eigen_columns[half][:1] + damping
-        scaled_region(z, half)[...] = (part_scatter.total(half) / divisor).astype(BF16)
-        scaled_gather.start(half)
-    scaled_gather.forward()
-    cov_scatter.forward()
-    scaled_gather.near()
-    scaled_gather.far()
+    scaled_gathers = []
+    for number, scatter in enumerate(part_scatters):
+        gather = Gather(
+            pool, lambda place, half, number=number: rows_of(scaled, place, half, number), z, z_up, z_down
+        )
+        for half in range(2):
+            scatter.arrived(half)
+            divisor = column * eigen_columns[half, :1, number * wave : (number + 1) * wave] + damping
+            rows_of(scaled, z, half, number)[...] = (scatter.total(half) / divisor).astype(BF16)
+            gather.start(half)
+        scaled_gathers.append(gather)
+        if number + 1 < WAVES:
+            if number + 2 == WAVES:
+                part_scatters[number + 1].add()
+            gather.forward()
 
     lines = rows // CHUNKS
-    half_width = width // 2
     half_lines = lines // 2
-    finishing = []
-    scatters = []
-    for chunk in range(CHUNKS):
-        chunk_rows = slice(chunk * lines, (chunk + 1) * lines)
-
+    crossings, sums, ends, to_core_last = [], [], [], []
+
+    def pass_to_core(ref):
+        to_core_last.append(Message(pool, ref, ref, core).start())
+
+    def start_sum(number):
         def partial(side, target):
             def one(place, unused):
-                left = basis[(place // 2) * 2 + side, chunk_rows, :]
-                target[place] = dot(left, scaled[lax.rem(place, 2)]).astype(target.dtype)
+                left = basis[(place // 2) * 2 + side]
+                right = scaled[lax.rem(place, 2), :, number * wave : (number + 1) * wave]
+                target[place] = dot(left, right).astype(target.dtype)
                 return unused
 
             lax.fori_loop(0, 4, one, 0)
 
-        partial(1 - c, away.at[chunk])
-        crossing = Message(pool, away.at[chunk], away_in.at[chunk], core).start()
-        finishing.append(crossing)
+        partial(1 - c, away.at[number])
+        crossings.append(Message(pool, away.at[number], away_in.at[number], core).start())
         partial(c, home)
-        crossing.arrived()
-        home_sum[chunk] = (home[...] + away_in[chunk].astype(F32)).astype(BF16)
-
-        def home_mine(place, half, chunk=chunk):
-            return home_sum.at[chunk, place, :, half * half_width : (half + 1) * half_width]
-
-        scatter = Scatter(
-            pool,
-            home_mine,
-            lambda half, chunk=chunk: home_transit.at[chunk, half],
-            lambda slot, chunk=chunk: home_slots.at[chunk, slot],
-            x,
-            x_up,
-            x_down,
-        )
-        scatter.start_far()
-        scatter.start_near()
-        scatters.append(scatter)
-
-    ends = []
-    for chunk in range(CHUNKS):
-        scatter = scatters[chunk]
-        scatter.forward()
+
+    def cross_sum(number, count):
+        crossings[number].arrived()
+        home_sum[number] = (home[...] + away_in[number].astype(F32)).astype(BF16)
+        size = rows // count // 2
+        for chunk in range(count):
+            sums.append(
+                Scatter(
+                    pool,
+                    lambda place, half, start=chunk * 2 * size: home_sum.at[
+                        number, place, start + half * size : start + (half + 1) * size, :
+                    ],
+                    lambda half, start=chunk * size: home_transit.at[number, half, start : start + size, :],
+                    lambda slot, start=chunk * size: home_slots.at[number, slot, start : start + size, :],
+                    x,
+                    x_up,
+                    x_down,
+                )
+            )
+
+    def finish_sum(scatter):
         scatter.arrived(0)
         scatter.arrived(1)
-        restored = jnp.concatenate([scatter.total(0), scatter.total(1)], axis=1).astype(BF16)
-        new = lax.dot_general(restored, basis_out_tile[...], (((1,), (1,)), ((), ())), preferred_element_type=F32)
-
-        def region(place, half, high, chunk=chunk):
+        return jnp.concatenate([scatter.total(0), scatter.total(1)], axis=0).astype(BF16)
+
+    for number, gather in enumerate(scaled_gathers):
+        gather.near()
+        gather.far()
+        start_sum(number)
+        if number + 1 < WAVES:
+            scaled_gathers[number + 1].forward()
+            cross_sum(number, 1)
+            sums[number].start_far()
+            sums[number].start_near()
+            if number + 2 == WAVES:
+                cov_scatter.add()
+        else:
+            for before in sums:
+                before.add()
+            cross_sum(number, CHUNKS)
+    last_sums = sums[WAVES - 1 :]
+    last_sums[0].start_far()
+    last_sums[0].start_near()
+    if CHUNKS > 1:
+        last_sums[1].start_far()
+    for number in range(WAVES - 1):
+        restored_part[:, number * wave : (number + 1) * wave] = finish_sum(sums[number])
+
+    def finish_chunk(chunk):
+        chunk_rows = slice(chunk * lines, (chunk + 1) * lines)
+        restored_part[chunk_rows, (WAVES - 1) * wave :] = finish_sum(last_sums[chunk])
+        new = lax.dot_general(
+            restored_part[chunk_rows, :],
+            basis_out_tile[...],
+            (((1,), (1,)), ((), ())),
+            preferred_element_type=F32,
+        )
+
+        def region(place, half, high):
             start = (high * 8 + place * 2 + c) * rows + chunk * lines
             if half is None:
                 return gathered.at[pl.ds(pl.multiple_of(start, 16), lines), :]
             return gathered.at[pl.ds(pl.multiple_of(start + half * half_lines, 16), half_lines), :]
 
-        own_gather = Gather(pool, functools.partial(region, high=xh), z, z_up, z_down)
-        other_gather = Gather(pool, functools.partial(region, high=1 - xh), z, z_up, z_down)
+        own = Gather(pool, functools.partial(region, high=xh), z, z_up, z_down)
+        other = Gather(pool, functools.partial(region, high=1 - xh), z, z_up, z_down)
         mine = region(z, None, xh)
         mine[...] = new.astype(BF16)
-        own_gather.start(0)
-        own_gather.start(1)
         across = Message(pool, mine, mine, x_far).start()
-        finishing += [across, Message(pool, mine, mine, core).start()]
-        ends.append((own_gather, other_gather, across, region))
+        own.start(0)
+        own.start(1)
+        pass_to_core(mine)
+        ends.append((own, other, across, region))
+
+    def start_other(chunk):
+        own, other, across, region = ends[chunk]
+        across.arrived()
+        other.start(0)
+        other.start(1)
+        pass_to_core(region(z, None, 1 - xh))
+
+    def forward(chunk, high):
+        gather = ends[chunk][high]
+        region = ends[chunk][3]
+        gather.forward()
+        gather.near()
+        for place in (above, below):
+            pass_to_core(region(place, None, xh if high == 0 else 1 - xh))
+
+    def last(chunk, high):
+        ends[chunk][high].far()
+        pass_to_core(ends[chunk][3](far, None, xh if high == 0 else 1 - xh))
+
+    last_sums[0].add()
+    for chunk in range(CHUNKS):
+        if chunk + 1 < CHUNKS:
+            last_sums[chunk + 1].start_near()
+        if chunk + 2 < CHUNKS:
+            last_sums[chunk + 2].start_far()
+        finish_chunk(chunk)
+        if chunk + 1 < CHUNKS:
+            last_sums[chunk + 1].add()
+        if chunk >= 1:
+            forward(chunk - 1, 0)
+            start_other(chunk - 1)
+        if chunk >= 2:
+            forward(chunk - 2, 1)
+    forward(CHUNKS - 1, 0)
+    start_other(CHUNKS - 1)
+    if CHUNKS > 1:
+        forward(CHUNKS - 2, 1)
 
     cov_scatter.arrived(0)
     cov_scatter.arrived(1)
-    totals = [cov_scatter.total(0), cov_scatter.total(1)]
-    cov[1 - xh, z] = jnp.where(xh == 0, totals[1], totals[0]).astype(BF16)
+    cov[1 - xh, z] = cov_scatter.total(1 - xh).astype(BF16)
     cov_message = Message(pool, cov.at[1 - xh, z], cov_across, x_far).start()
 
-    to_core_last = []
-    for own_gather, other_gather, across, region in ends:
-        across.arrived()
-        other_gather.start(0)
-        other_gather.start(1)
-        received = region(z, None, 1 - xh)
-        to_core_last.append(Message(pool, received, received, core).start())
-    for own_gather, other_gather, across, region in ends:
-        for gather, high in ((own_gather, xh), (other_gather, 1 - xh)):
-            gather.forward()
-            gather.near()
-            for place in (above, below):
-                received = region(place, None, high)
-                to_core_last.append(Message(pool, received, received, core).start())
-
+    forward(CHUNKS - 1, 1)
+    for chunk in range(CHUNKS):
+        last(chunk, 0)
+    total = cov_scatter.total(xh)
+    for chunk in range(CHUNKS):
+        last(chunk, 1)
     cov_message.arrived()
-    total = jnp.where(xh == 0, totals[0], totals[1]) + cov_across[...].astype(F32)
+    total = total + cov_across[...].astype(F32)
     in_cov[...] = total[:rows]
     out_cov[...] = total[rows:]
 
-    for own_gather, other_gather, across, region in ends:
-        for gather, high in ((own_gather, xh), (other_gather, 1 - xh)):
-            gather.far()
-            received = region(far, None, high)
-            to_core_last.append(Message(pool, received, received, core).start())
-
     for message in to_core_last:
         message.arrived()
-    for own_gather, other_gather, across, region in ends:
-        own_gather.sent()
-        other_gather.sent()
-    for chunk, message in enumerate(finishing[CHUNKS:]):
-        if chunk % 2 == 1:
-            message.arrived()
-    for message in finishing + to_core_last + scatter_basis + small + turned_core:
+    for own, other, across, region in ends:
+        own.sent()
+        other.sent()
+        across.sent()
+    for message in crossings + to_core_last + list(scatter_basis.values()) + small + turned_core:
         message.sent()
     for message in list(token_messages.values()) + [column_message, grad_message, cov_message]:
         message.sent()
-    for group in [turned_gather, basis_gather, scaled_gather, cov_scatter, part_scatter] + scatters:
+    for group in [turned_gather, basis_gather, cov_scatter] + part_scatters + scaled_gathers + sums:
         group.sent()
 
 
-def finish(gathered, in_cov, out_cov, old_in, old_out, precond, in_factor, out_factor, sem, tokens):
-    copy = pltpu.make_async_copy(gathered, precond, sem)
-    copy.start()
-    in_factor[...] = factor_decay * old_in[...] + (1.0 - factor_decay) * in_cov[...] / tokens
-    out_factor[...] = factor_decay * old_out[...] + (1.0 - factor_decay) * out_cov[...] / tokens
-    copy.wait()
+def finish(gathered, in_cov, out_cov, old_in, old_out, precond, in_factor, out_factor, new_in, new_out, sem, tokens):
+    copies = [pltpu.make_async_copy(gathered, precond, sem.at[0])]
+    copies[0].start()
+    new_in[...] = factor_decay * old_in[...] + (1.0 - factor_decay) * in_cov[...] / tokens
+    new_out[...] = factor_decay * old_out[...] + (1.0 - factor_decay) * out_cov[...] / tokens
+    copies += [pltpu.make_async_copy(new_in, in_factor, sem.at[1])]
+    copies += [pltpu.make_async_copy(new_out, out_factor, sem.at[2])]
+    for copy in copies[1:]:
+        copy.start()
+    for copy in copies:
+        copy.wait()
 
 
 def shards(
@@ -534,7 +610,6 @@
     out_rows = old_out_factor.shape[0]
     deep = rows + out_rows
     total = 16 * rows
-    lines = rows // CHUNKS
     narrow = width // 4
     anywhere = pl.BlockSpec(memory_space=pl.ANY)
     vmem = pl.BlockSpec(memory_space=pltpu.VMEM)
@@ -542,17 +617,18 @@
         pltpu.VMEM((4, rows, 2 * rows), BF16),
         pltpu.VMEM((2, 4, rows, width), BF16),
         pltpu.VMEM((2, 4 * narrow, width), BF16),
-        pltpu.VMEM((2, narrow, width), BF16),
-        pltpu.VMEM((4, narrow, width), BF16),
+        pltpu.VMEM((WAVES, 2, narrow, width // WAVES), BF16),
+        pltpu.VMEM((WAVES, 4, narrow, width // WAVES), BF16),
         pltpu.VMEM((2, 4 * narrow, width), BF16),
         pltpu.VMEM((4, 8, rows), F32),
         pltpu.VMEM((2, 8, width), F32),
-        pltpu.VMEM((CHUNKS, 4, lines, width), BF16),
-        pltpu.VMEM((CHUNKS, 4, lines, width), BF16),
-        pltpu.VMEM((4, lines, width), F32),
-        pltpu.VMEM((CHUNKS, 4, lines, width), BF16),
-        pltpu.VMEM((CHUNKS, 2, lines, width // 2), BF16),
-        pltpu.VMEM((CHUNKS, 4, lines, width // 2), BF16),
+        pltpu.VMEM((WAVES, 4, rows, width // WAVES), BF16),
+        pltpu.VMEM((WAVES, 4, rows, width // WAVES), BF16),
+        pltpu.VMEM((4, rows, width // WAVES), F32),
+        pltpu.VMEM((WAVES, 4, rows, width // WAVES), BF16),
+        pltpu.VMEM((rows, width), BF16),
+        pltpu.VMEM((WAVES, 2, rows // 2, width // WAVES), BF16),
+        pltpu.VMEM((WAVES, 4, rows // 2, width // WAVES), BF16),
         pltpu.VMEM((2, 8, tokens, rows), BF16),
         pltpu.VMEM((2, tokens, width), BF16),
         pltpu.VMEM((2, tokens, width), BF16),
@@ -571,8 +647,8 @@
         kernel,
         out_shape=(
             pltpu.VMEM((total, width), BF16),
-            jax.ShapeDtypeStruct((rows, width), F32),
-            jax.ShapeDtypeStruct((out_rows, width), F32),
+            pltpu.VMEM((rows, width), F32),
+            pltpu.VMEM((out_rows, width), F32),
         ),
         in_specs=[anywhere] * 5 + [vmem] * 2,
         out_specs=(vmem, vmem, vmem),
@@ -588,8 +664,8 @@
         kernel_grad,
         basis_in,
         basis_out,
-        jnp.broadcast_to(eigen_in[None, :], (8, rows)),
-        jnp.broadcast_to(eigen_out[None, :], (8, width)),
+        eigen_in,
+        eigen_out,
     )
     return pl.pallas_call(
         functools.partial(finish, tokens=16 * tokens),
@@ -599,8 +675,8 @@
             jax.ShapeDtypeStruct((out_rows, width), F32),
         ),
         in_specs=[vmem] * 5,
-        out_specs=(anywhere, vmem, vmem),
-        scratch_shapes=[pltpu.SemaphoreType.DMA],
+        out_specs=(anywhere, anywhere, anywhere),
+        scratch_shapes=[pltpu.VMEM((rows, width), F32), pltpu.VMEM((out_rows, width), F32), pltpu.SemaphoreType.DMA((3,))],
         compiler_params=pltpu.CompilerParams(vmem_limit_bytes=40 * 2**20),
         name="finish",
     )(gathered, in_cov, out_cov, old_in_factor, old_out_factor)

time: 178 us -> 158 us (0.89)
  Pallas kernels: 173 us -> 157 us
  local copies, waits for them, and re-layouts: 4.76 us -> 0.01 us
    pallas_call x1, Pallas kernels: 168 us -> 153 us  [shards(): pl.pallas_call(kernel, out_shape=(pltpu.VMEM((total, width), BF16), pltpu...]
    broadcast_in_dim x2 -> x0, local copies, waits for them, and re-layouts: 2.58 us -> none  [the longest x1 1.3 us: shards(): jnp.broadcast_to(eigen_out[None, :], (8, width))]
    unnamed x8 -> x4, local copies, waits for them, and re-layouts: 2.18 us -> 0.01 us
where the time goes in v2:
time: 158 us
  Pallas kernels  157 us (99%)
    pallas_call x1, Pallas kernels, shards(): pl.pallas_call(kernel, out_shape=(pltpu.VMEM((total, width), BF16), pltpu...  153 us
    pallas_call x1, Pallas kernels, shards(): pl.pallas_call(functools.partial(finish, tokens=16 * tokens), out_shape=(...  4.15 us

profile of v2, /device:TPU:1, one launch (start us, length us, event | category | flops | bytes accessed | tf_op | source)
XLA Modules:
  0.0 158.0 jit_solution(9533765789081536945)
XLA Ops:
  0.6 0.0 copy-start.1
  0.6 0.0 copy-start
  0.7 153.0 %precondition.1 = (bf16[6144,768]{1,0:T(8,128)(2,1)S(1)}, f32[384,768]{1,0:T(8,128)S(1)}, f32[48,768]{1,0:T(8,128)S(1)}) custom-call(bf16[512,6144]{1,0:T(8,128)(2,1)} %inputs.1, bf16[512,6144]{1,0:T(8,128)(2,1)} %grads.1, bf16[384,768]{1,0:T(8,128)(2,1)} %kernel_grad.1, bf16[48,6144]{1,0:T(8,128)(2,1)} %basis_in.1, bf16[768,768]{1,0:T(8,128)(2,1)} %basis_out.1, ...), custom_call_target="tpu_custom_call" | custom-call | flops 20000000000 | bytes 40000000 | tf_op jit(solution)/shard_map/precondition/pallas_call | solution.py:646
  153.7 0.0 copy-done.1
  153.7 0.0 copy-done
  153.7 4.2 %finish.1 = (bf16[6144,768]{1,0:T(8,128)(2,1)}, f32[384,768]{1,0:T(8,128)}, f32[48,768]{1,0:T(8,128)}) custom-call(bf16[6144,768]{1,0:T(8,128)(2,1)S(1)} %get-tuple-element.6.gathered, f32[384,768]{1,0:T(8,128)S(1)} %get-tuple-element.7.in_cov, f32[48,768]{1,0:T(8,128)S(1)} %get-tuple-element.8.out_cov, f32[384,768]{1,0:T(8,128)S(1)} %copy-done, ...), custom_call_target="tpu_custom_call" | custom-call | tf_op jit(solution)/shard_map/finish/pallas_call | solution.py:670
Async XLA Ops:
  0.6 153.1 %copy-start.1 = (f32[48,768]{1,0:T(8,128)S(1)}, f32[48,768]{1,0:T(8,128)}, u32[]{:S(2)}) copy-start(f32[48,768]{1,0:T(8,128)} %old_out.1) | copy-start | bytes 442372
  0.6 153.1 %copy-start = (f32[384,768]{1,0:T(8,128)S(1)}, f32[384,768]{1,0:T(8,128)}, u32[]{:S(2)}) copy-start(f32[384,768]{1,0:T(8,128)} %old_in.1) | copy-start | bytes 3538948

commit v3 on v2

--- a/solution.py
+++ b/solution.py
@@ -29,6 +29,7 @@
     def __init__(self, pool, source, target, to):
         number = pool[2]
         pool[2] += 1
+        self.sems = (pool[0].at[number], pool[1].at[number])
         self.copy = pltpu.make_async_remote_copy(
             src_ref=source,
             dst_ref=target,
@@ -174,6 +175,10 @@
     cov_transit,
     cov_slots,
     cov_across,
+    strips_part,
+    strips,
+    settled,
+    swapped,
     grad_tile,
     basis_out_tile,
     local,
@@ -227,6 +232,27 @@
     for partner in partners:
         pl.semaphore_signal(barrier, inc=1, device_id=partner, device_id_type=MESH)
 
+    row = xh * 4 + z
+    diagonal = row == owner
+
+    def on_diagonal(row, c):
+        return (row // 4) * 8 + lax.rem(row, 4) * 2 + c, owner
+
+    mirror = [((owner // 4) * 8 + lax.rem(owner, 4) * 2 + side, row) for side in range(2)]
+
+    @pl.when(diagonal)
+    def _():
+        for step in range(1, 8):
+            pl.semaphore_signal(
+                barrier, inc=1, device_id=on_diagonal(lax.rem(row + step, 8), c), device_id_type=MESH
+            )
+
+    @pl.when(jnp.logical_not(diagonal))
+    def _():
+        for to in mirror + [on_diagonal(owner, c)]:
+            pl.semaphore_signal(barrier, inc=1, device_id=to, device_id_type=MESH)
+
+
     def strip_rows(x, y, c):
         block = (x // 2) * 2 + c
         start = pl.multiple_of((y * 2 + lax.rem(x, 2)) * strip, strip)
@@ -251,7 +277,7 @@
                 block_columns(inputs, high * 8 + order[step] * 2 + c), tokens.at[0, step * 2 + high]
             )
 
-    pl.semaphore_wait(barrier, len(partners))
+    pl.semaphore_wait(barrier, len(partners) + jnp.where(diagonal, 7, 3))
 
     scatter_basis = {}
     for step, side in plane:
@@ -333,6 +359,16 @@
         dot_rows(grad_columns[0], grad_columns[0]) + dot_rows(grad_columns[1], grad_columns[1])
     ).astype(BF16)
 
+    def half_columns(number, side):
+        return token_columns[number, :, pl.ds(pl.multiple_of(side * rows, rows), rows)]
+
+    strips_part[...] = (
+        dot_rows(half_columns(0, c), half_columns(0, 1 - c)) + dot_rows(half_columns(1, c), half_columns(1, 1 - c))
+    ).astype(BF16)
+
+    def own_side(row):
+        return jnp.where(row <= owner, c, 1 - c)
+
     def cov_product(step):
         for high in range(2):
             got_tokens[step, high].wait()
@@ -340,11 +376,15 @@
         place = order[step]
 
         def product(high, unused):
-            tile = dot_rows(tokens[0, step * 2 + high], token_columns[0])
-            tile = tile + dot_rows(tokens[1, step * 2 + high], token_columns[1])
+            side = own_side(high * 4 + place)
+            tile = dot_rows(tokens[0, step * 2 + high], half_columns(0, side))
+            tile = tile + dot_rows(tokens[1, step * 2 + high], half_columns(1, side))
             cov[high, place, :rows] = tile.astype(BF16)
             start = pl.multiple_of((high * 8 + place * 2 + c) * out_rows, out_rows)
-            cov[high, place, rows:] = grad_part[pl.ds(start, out_rows), :]
+            cov[high, place, rows : rows + out_rows] = grad_part[pl.ds(start, out_rows), :rows]
+            cov[high, place, rows + out_rows : rows + 2 * out_rows] = grad_part[pl.ds(start, out_rows), rows:]
+            start = pl.multiple_of((high * 4 + place) * out_rows, out_rows)
+            cov[high, place, rows + 2 * out_rows :] = strips_part[pl.ds(start, out_rows), :]
             return unused
 
         lax.fori_loop(0, 2, product, 0)
@@ -359,6 +399,7 @@
     cov_product(2)
     cov_scatter.start_near()
     cov_product(3)
+    cov_scatter.add()
     turned_gather.far()
     turned_core.append(to_core(2))
     basis_gather.near()
@@ -403,6 +444,11 @@
             part_scatters[number - 1].add()
         rotate(z // 2, number)
         scatter.start_near()
+
+    cov_scatter.arrived(0)
+    cov_scatter.arrived(1)
+    cov[1 - xh, z] = cov_scatter.total(1 - xh).astype(BF16)
+    cov_message = Message(pool, cov.at[1 - xh, z], cov_across, x_far).start()
 
     for message in small:
         message.arrived()
@@ -425,6 +471,35 @@
             if number + 2 == WAVES:
                 part_scatters[number + 1].add()
             gather.forward()
+
+    cov_message.arrived()
+    total = cov_scatter.total(xh) + cov_across[...].astype(F32)
+    settled[...] = total.astype(BF16)
+    out_cov[:, :rows] = total[rows : rows + out_rows]
+    out_cov[:, rows:] = total[rows + out_rows : rows + 2 * out_rows]
+    side = own_side(row)
+    own_half = pl.ds(pl.multiple_of(side * rows, rows), rows)
+    other_half = pl.ds(pl.multiple_of((1 - side) * rows, rows), rows)
+    in_cov[:, own_half] = total[:rows]
+    my_strip = pl.ds(pl.multiple_of(row * out_rows, out_rows), out_rows)
+    mirror_core = jnp.where(row < owner, c, 1 - c)
+    swap = Message(pool, settled.at[:rows], swapped, (mirror[0][0] + mirror_core, row))
+    strip_message = Message(
+        pool, settled.at[rows + 2 * out_rows :], strips.at[my_strip, :], on_diagonal(owner, c)
+    )
+    seven_wait = pltpu.make_async_remote_copy(
+        src_ref=strips.at[: 7 * out_rows],
+        dst_ref=strips.at[: 7 * out_rows],
+        send_sem=strip_message.sems[0],
+        recv_sem=strip_message.sems[1],
+        device_id=on_diagonal(owner, c),
+        device_id_type=MESH,
+    )
+
+    @pl.when(jnp.logical_not(diagonal))
+    def _():
+        swap.start()
+        strip_message.start()
 
     lines = rows // CHUNKS
     half_lines = lines // 2
@@ -480,8 +555,6 @@
             cross_sum(number, 1)
             sums[number].start_far()
             sums[number].start_near()
-            if number + 2 == WAVES:
-                cov_scatter.add()
         else:
             for before in sums:
                 before.add()
@@ -558,21 +631,25 @@
     if CHUNKS > 1:
         forward(CHUNKS - 2, 1)
 
-    cov_scatter.arrived(0)
-    cov_scatter.arrived(1)
-    cov[1 - xh, z] = cov_scatter.total(1 - xh).astype(BF16)
-    cov_message = Message(pool, cov.at[1 - xh, z], cov_across, x_far).start()
-
     forward(CHUNKS - 1, 1)
     for chunk in range(CHUNKS):
         last(chunk, 0)
-    total = cov_scatter.total(xh)
+
+    @pl.when(diagonal)
+    def _():
+        strips[my_strip, :] = settled[rows + 2 * out_rows :]
+        seven_wait.wait_recv()
+        in_cov[:, other_half] = strips[...].astype(F32)
+
+    @pl.when(jnp.logical_not(diagonal))
+    def _():
+        swap.arrived()
+        in_cov[:, other_half] = jnp.transpose(swapped[...].astype(F32))
+        swap.sent()
+        strip_message.sent()
+
     for chunk in range(CHUNKS):
         last(chunk, 1)
-    cov_message.arrived()
-    total = total + cov_across[...].astype(F32)
-    in_cov[...] = total[:rows]
-    out_cov[...] = total[rows:]
 
     for message in to_core_last:
         message.arrived()
@@ -608,7 +685,7 @@
     strip = basis_in.shape[0]
     tokens = inputs.shape[0]
     out_rows = old_out_factor.shape[0]
-    deep = rows + out_rows
+    deep = rows + 3 * out_rows
     total = 16 * rows
     narrow = width // 4
     anywhere = pl.BlockSpec(memory_space=pl.ANY)
@@ -633,10 +710,14 @@
         pltpu.VMEM((2, tokens, width), BF16),
         pltpu.VMEM((2, tokens, width), BF16),
         pltpu.VMEM((width, width), BF16),
-        pltpu.VMEM((2, 4, deep, width), BF16),
-        pltpu.VMEM((2, deep, width), BF16),
-        pltpu.VMEM((4, deep, width), BF16),
-        pltpu.VMEM((deep, width), BF16),
+        pltpu.VMEM((2, 4, deep, rows), BF16),
+        pltpu.VMEM((2, deep, rows), BF16),
+        pltpu.VMEM((4, deep, rows), BF16),
+        pltpu.VMEM((deep, rows), BF16),
+        pltpu.VMEM((rows, rows), BF16),
+        pltpu.VMEM((rows, rows), BF16),
+        pltpu.VMEM((deep, rows), BF16),
+        pltpu.VMEM((rows, rows), BF16),
         pltpu.VMEM((rows, width), BF16),
         pltpu.VMEM((width, width), BF16),
         pltpu.SemaphoreType.DMA((16,)),

time: 158 us -> 171 us (1.082)
  Pallas kernels: 157 us -> 171 us
    pallas_call x1, Pallas kernels: 153 us -> 166 us  [shards(): pl.pallas_call(kernel, out_shape=(pltpu.VMEM((total, width), BF16), pltpu...]
where the time goes in v3:
time: 171 us
  Pallas kernels  171 us (100%)
    pallas_call x1, Pallas kernels, shards(): pl.pallas_call(kernel, out_shape=(pltpu.VMEM((total, width), BF16), pltpu...  166 us
    pallas_call x1, Pallas kernels, shards(): pl.pallas_call(functools.partial(finish, tokens=16 * tokens), out_shape=(...  4.15 us

profile of v3, /device:TPU:1, one launch (start us, length us, event | category | flops | bytes accessed | tf_op | source)
XLA Modules:
  0.0 171.2 jit_solution(12043891154745898612)
XLA Ops:
  0.6 0.0 copy-start.1
  0.6 0.0 copy-start
  0.7 166.4 %precondition.1 = (bf16[6144,768]{1,0:T(8,128)(2,1)S(1)}, f32[384,768]{1,0:T(8,128)S(1)}, f32[48,768]{1,0:T(8,128)S(1)}) custom-call(bf16[512,6144]{1,0:T(8,128)(2,1)} %inputs.1, bf16[512,6144]{1,0:T(8,128)(2,1)} %grads.1, bf16[384,768]{1,0:T(8,128)(2,1)} %kernel_grad.1, bf16[48,6144]{1,0:T(8,128)(2,1)} %basis_in.1, bf16[768,768]{1,0:T(8,128)(2,1)} %basis_out.1, ...), custom_call_target="tpu_custom_call" | custom-call | flops 20000000000 | bytes 40000000 | tf_op jit(solution)/shard_map/precondition/pallas_call | solution.py:727
  167.0 0.0 copy-done.1
  167.0 0.0 copy-done
  167.0 4.2 %finish.1 = (bf16[6144,768]{1,0:T(8,128)(2,1)}, f32[384,768]{1,0:T(8,128)}, f32[48,768]{1,0:T(8,128)}) custom-call(bf16[6144,768]{1,0:T(8,128)(2,1)S(1)} %get-tuple-element.6.gathered, f32[384,768]{1,0:T(8,128)S(1)} %get-tuple-element.7.in_cov, f32[48,768]{1,0:T(8,128)S(1)} %get-tuple-element.8.out_cov, f32[384,768]{1,0:T(8,128)S(1)} %copy-done, ...), custom_call_target="tpu_custom_call" | custom-call | tf_op jit(solution)/shard_map/finish/pallas_call | solution.py:751
Async XLA Ops:
  0.6 166.4 %copy-start.1 = (f32[48,768]{1,0:T(8,128)S(1)}, f32[48,768]{1,0:T(8,128)}, u32[]{:S(2)}) copy-start(f32[48,768]{1,0:T(8,128)} %old_out.1) | copy-start | bytes 442372
  0.6 166.4 %copy-start = (f32[384,768]{1,0:T(8,128)S(1)}, f32[384,768]{1,0:T(8,128)}, u32[]{:S(2)}) copy-start(f32[384,768]{1,0:T(8,128)} %old_in.1) | copy-start | bytes 3538948

commit v4 on v2

--- a/solution.py
+++ b/solution.py
@@ -174,6 +174,10 @@
     cov_transit,
     cov_slots,
     cov_across,
+    right,
+    right_in,
+    right_transit,
+    right_slots,
     grad_tile,
     basis_out_tile,
     local,
@@ -271,6 +275,7 @@
 
     token_messages = {}
     column_message = Message(pool, owner_columns(inputs), token_columns.at[1], core).start()
+    grad_message = Message(pool, owner_columns(grads), grad_columns.at[1], core).start()
     for step in range(4):
         for high in range(2):
             token_messages[step, high] = Message(
@@ -279,7 +284,6 @@
                 tokens.at[1, step * 2 + high],
                 core,
             ).start()
-    grad_message = Message(pool, owner_columns(grads), grad_columns.at[1], core).start()
 
     got_grad.wait()
     got_basis_out.wait()
@@ -312,18 +316,19 @@
             message.arrived()
     basis_gather.start(0)
     turned_gather.start(0)
-    for (step, side, t), message in scatter_basis.items():
-        if step not in (-1, 0):
-            message.arrived()
-    basis_gather.start(1)
-    turned_gather.start(1)
-    turned_core = [to_core(0)]
-
     def cov_mine(place, half):
         return cov.at[half, place]
 
     cov_scatter = Scatter(
         pool, cov_mine, lambda half: cov_transit.at[half], lambda slot: cov_slots.at[slot], z, z_up, z_down
+    )
+    half_rows = rows // 2
+
+    def right_mine(place, half):
+        return right.at[xh, place, half * half_rows : (half + 1) * half_rows, :]
+
+    right_scatter = Scatter(
+        pool, right_mine, lambda half: right_transit.at[half], lambda slot: right_slots.at[slot], z, z_up, z_down
     )
     got_columns.wait()
     got_grad_columns.wait()
@@ -342,23 +347,33 @@
         def product(high, unused):
             tile = dot_rows(tokens[0, step * 2 + high], token_columns[0])
             tile = tile + dot_rows(tokens[1, step * 2 + high], token_columns[1])
-            cov[high, place, :rows] = tile.astype(BF16)
+            cov[high, place, :rows] = tile[:, :rows].astype(BF16)
+            right[high, place] = tile[:, rows:].astype(BF16)
             start = pl.multiple_of((high * 8 + place * 2 + c) * out_rows, out_rows)
-            cov[high, place, rows:] = grad_part[pl.ds(start, out_rows), :]
+            cov[high, place, rows : rows + out_rows] = grad_part[pl.ds(start, out_rows), :rows]
+            cov[high, place, rows + out_rows :] = grad_part[pl.ds(start, out_rows), rows:]
             return unused
 
         lax.fori_loop(0, 2, product, 0)
 
     cov_product(0)
     cov_scatter.start_far()
-    turned_gather.forward()
-    turned_gather.near()
-    turned_core += [to_core(1), to_core(3)]
-    basis_gather.forward()
+    for (step, side, t), message in scatter_basis.items():
+        if step not in (-1, 0):
+            message.arrived()
+    basis_gather.start(1)
+    turned_gather.start(1)
+    turned_core = [to_core(0)]
     cov_product(1)
     cov_product(2)
     cov_scatter.start_near()
+    turned_gather.forward()
+    basis_gather.forward()
     cov_product(3)
+    turned_gather.near()
+    turned_core += [to_core(1), to_core(3)]
+    right_message = Message(pool, right.at[1 - xh], right_in, x_far).start()
+    cov_scatter.add()
     turned_gather.far()
     turned_core.append(to_core(2))
     basis_gather.near()
@@ -403,6 +418,11 @@
             part_scatters[number - 1].add()
         rotate(z // 2, number)
         scatter.start_near()
+
+    cov_scatter.arrived(0)
+    cov_scatter.arrived(1)
+    cov[1 - xh, z] = cov_scatter.total(1 - xh).astype(BF16)
+    cov_message = Message(pool, cov.at[1 - xh, z], cov_across, x_far).start()
 
     for message in small:
         message.arrived()
@@ -433,66 +453,76 @@
     def pass_to_core(ref):
         to_core_last.append(Message(pool, ref, ref, core).start())
 
-    def start_sum(number):
+    def start_sum(number, start, size):
+        chunk_rows = slice(start, start + size)
+
         def partial(side, target):
             def one(place, unused):
-                left = basis[(place // 2) * 2 + side]
+                left = basis[(place // 2) * 2 + side, chunk_rows, :]
                 right = scaled[lax.rem(place, 2), :, number * wave : (number + 1) * wave]
-                target[place] = dot(left, right).astype(target.dtype)
+                target[place, chunk_rows, :] = dot(left, right).astype(target.dtype)
                 return unused
 
             lax.fori_loop(0, 4, one, 0)
 
         partial(1 - c, away.at[number])
-        crossings.append(Message(pool, away.at[number], away_in.at[number], core).start())
+        crossing = Message(
+            pool, away.at[number, :, chunk_rows, :], away_in.at[number, :, chunk_rows, :], core
+        ).start()
+        crossings.append(crossing)
         partial(c, home)
 
-    def cross_sum(number, count):
-        crossings[number].arrived()
-        home_sum[number] = (home[...] + away_in[number].astype(F32)).astype(BF16)
-        size = rows // count // 2
-        for chunk in range(count):
-            sums.append(
-                Scatter(
-                    pool,
-                    lambda place, half, start=chunk * 2 * size: home_sum.at[
-                        number, place, start + half * size : start + (half + 1) * size, :
-                    ],
-                    lambda half, start=chunk * size: home_transit.at[number, half, start : start + size, :],
-                    lambda slot, start=chunk * size: home_slots.at[number, slot, start : start + size, :],
-                    x,
-                    x_up,
-                    x_down,
-                )
+        def cross():
+            crossing.arrived()
+            home_sum[number, :, chunk_rows, :] = (
+                home[:, chunk_rows, :] + away_in[number, :, chunk_rows, :].astype(F32)
+            ).astype(BF16)
+            half = size // 2
+            scatter = Scatter(
+                pool,
+                lambda place, part_of: home_sum.at[
+                    number, place, start + part_of * half : start + (part_of + 1) * half, :
+                ],
+                lambda part_of: home_transit.at[number, part_of, start // 2 : start // 2 + half, :],
+                lambda slot: home_slots.at[number, slot, start // 2 : start // 2 + half, :],
+                x,
+                x_up,
+                x_down,
             )
+            scatter.start_far()
+            scatter.start_near()
+            sums.append(scatter)
+
+        return cross
 
     def finish_sum(scatter):
         scatter.arrived(0)
         scatter.arrived(1)
         return jnp.concatenate([scatter.total(0), scatter.total(1)], axis=0).astype(BF16)
 
-    for number, gather in enumerate(scaled_gathers):
-        gather.near()
-        gather.far()
-        start_sum(number)
-        if number + 1 < WAVES:
-            scaled_gathers[number + 1].forward()
-            cross_sum(number, 1)
-            sums[number].start_far()
-            sums[number].start_near()
-            if number + 2 == WAVES:
-                cov_scatter.add()
-        else:
-            for before in sums:
-                before.add()
-            cross_sum(number, CHUNKS)
-    last_sums = sums[WAVES - 1 :]
-    last_sums[0].start_far()
-    last_sums[0].start_near()
-    if CHUNKS > 1:
-        last_sums[1].start_far()
-    for number in range(WAVES - 1):
-        restored_part[:, number * wave : (number + 1) * wave] = finish_sum(sums[number])
+    right_message.arrived()
+    right[xh] = (right[xh].astype(F32) + right_in[...].astype(F32)).astype(BF16)
+
+    scaled_gathers[0].near()
+    scaled_gathers[0].far()
+    cross = start_sum(0, 0, rows)
+    scaled_gathers[1].forward()
+    cross()
+    right_scatter.start_far()
+    right_scatter.start_near()
+    sums[0].add()
+    scaled_gathers[1].near()
+    scaled_gathers[1].far()
+    crosses = [start_sum(1, 0, lines)]
+    for chunk in range(CHUNKS):
+        if chunk + 1 < CHUNKS:
+            crosses.append(start_sum(1, (chunk + 1) * lines, lines))
+        crosses[chunk]()
+        if chunk == 1:
+            right_scatter.add()
+            sums[1].add()
+    restored_part[:, :wave] = finish_sum(sums[0])
+    last_sums = sums[1:]
 
     def finish_chunk(chunk):
         chunk_rows = slice(chunk * lines, (chunk + 1) * lines)
@@ -539,12 +569,7 @@
         ends[chunk][high].far()
         pass_to_core(ends[chunk][3](far, None, xh if high == 0 else 1 - xh))
 
-    last_sums[0].add()
     for chunk in range(CHUNKS):
-        if chunk + 1 < CHUNKS:
-            last_sums[chunk + 1].start_near()
-        if chunk + 2 < CHUNKS:
-            last_sums[chunk + 2].start_far()
         finish_chunk(chunk)
         if chunk + 1 < CHUNKS:
             last_sums[chunk + 1].add()
@@ -558,21 +583,19 @@
     if CHUNKS > 1:
         forward(CHUNKS - 2, 1)
 
-    cov_scatter.arrived(0)
-    cov_scatter.arrived(1)
-    cov[1 - xh, z] = cov_scatter.total(1 - xh).astype(BF16)
-    cov_message = Message(pool, cov.at[1 - xh, z], cov_across, x_far).start()
-
     forward(CHUNKS - 1, 1)
     for chunk in range(CHUNKS):
         last(chunk, 0)
-    total = cov_scatter.total(xh)
+    cov_message.arrived()
+    total = cov_scatter.total(xh) + cov_across[...].astype(F32)
+    in_cov[:, :rows] = total[:rows]
+    out_cov[:, :rows] = total[rows : rows + out_rows]
+    out_cov[:, rows:] = total[rows + out_rows :]
+    for half in range(2):
+        right_scatter.arrived(half)
+        in_cov[half * half_rows : (half + 1) * half_rows, rows:] = right_scatter.total(half)
     for chunk in range(CHUNKS):
         last(chunk, 1)
-    cov_message.arrived()
-    total = total + cov_across[...].astype(F32)
-    in_cov[...] = total[:rows]
-    out_cov[...] = total[rows:]
 
     for message in to_core_last:
         message.arrived()
@@ -582,9 +605,9 @@
         across.sent()
     for message in crossings + to_core_last + list(scatter_basis.values()) + small + turned_core:
         message.sent()
-    for message in list(token_messages.values()) + [column_message, grad_message, cov_message]:
+    for message in list(token_messages.values()) + [column_message, grad_message, cov_message, right_message]:
         message.sent()
-    for group in [turned_gather, basis_gather, cov_scatter] + part_scatters + scaled_gathers + sums:
+    for group in [turned_gather, basis_gather, cov_scatter, right_scatter] + part_scatters + scaled_gathers + sums:
         group.sent()
 
 
@@ -608,7 +631,7 @@
     strip = basis_in.shape[0]
     tokens = inputs.shape[0]
     out_rows = old_out_factor.shape[0]
-    deep = rows + out_rows
+    deep = rows + 2 * out_rows
     total = 16 * rows
     narrow = width // 4
     anywhere = pl.BlockSpec(memory_space=pl.ANY)
@@ -633,10 +656,14 @@
         pltpu.VMEM((2, tokens, width), BF16),
         pltpu.VMEM((2, tokens, width), BF16),
         pltpu.VMEM((width, width), BF16),
-        pltpu.VMEM((2, 4, deep, width), BF16),
-        pltpu.VMEM((2, deep, width), BF16),
-        pltpu.VMEM((4, deep, width), BF16),
-        pltpu.VMEM((deep, width), BF16),
+        pltpu.VMEM((2, 4, deep, rows), BF16),
+        pltpu.VMEM((2, deep, rows), BF16),
+        pltpu.VMEM((4, deep, rows), BF16),
+        pltpu.VMEM((deep, rows), BF16),
+        pltpu.VMEM((2, 4, rows, rows), BF16),
+        pltpu.VMEM((4, rows, rows), BF16),
+        pltpu.VMEM((2, rows // 2, rows), BF16),
+        pltpu.VMEM((4, rows // 2, rows), BF16),
         pltpu.VMEM((rows, width), BF16),
         pltpu.VMEM((width, width), BF16),
         pltpu.SemaphoreType.DMA((16,)),

time: 158 us -> 152 us (0.962)
  Pallas kernels: 157 us -> 151 us
    pallas_call x1, Pallas kernels: 153 us -> 147 us  [shards(): pl.pallas_call(kernel, out_shape=(pltpu.VMEM((total, width), BF16), pltpu...]
where the time goes in v4:
time: 152 us
  Pallas kernels  151 us (99%)
    pallas_call x1, Pallas kernels, shards(): pl.pallas_call(kernel, out_shape=(pltpu.VMEM((total, width), BF16), pltpu...  147 us
    pallas_call x1, Pallas kernels, shards(): pl.pallas_call(functools.partial(finish, tokens=16 * tokens), out_shape=(...  4.15 us

profile of v4, /device:TPU:1, one launch (start us, length us, event | category | flops | bytes accessed | tf_op | source)
XLA Modules:
  0.0 152.2 jit_solution(8182008059346594282)
XLA Ops:
  0.6 0.0 copy-start.1
  0.6 0.0 copy-start
  0.7 147.2 %precondition.1 = (bf16[6144,768]{1,0:T(8,128)(2,1)S(1)}, f32[384,768]{1,0:T(8,128)S(1)}, f32[48,768]{1,0:T(8,128)S(1)}) custom-call(bf16[512,6144]{1,0:T(8,128)(2,1)} %inputs.1, bf16[512,6144]{1,0:T(8,128)(2,1)} %grads.1, bf16[384,768]{1,0:T(8,128)(2,1)} %kernel_grad.1, bf16[48,6144]{1,0:T(8,128)(2,1)} %basis_in.1, bf16[768,768]{1,0:T(8,128)(2,1)} %basis_out.1, ...), custom_call_target="tpu_custom_call" | custom-call | flops 20000000000 | bytes 40000000 | tf_op jit(solution)/shard_map/precondition/pallas_call | solution.py:673
  147.9 0.0 copy-done.1
  147.9 0.0 copy-done
  147.9 4.2 %finish.1 = (bf16[6144,768]{1,0:T(8,128)(2,1)}, f32[384,768]{1,0:T(8,128)}, f32[48,768]{1,0:T(8,128)}) custom-call(bf16[6144,768]{1,0:T(8,128)(2,1)S(1)} %get-tuple-element.6.gathered, f32[384,768]{1,0:T(8,128)S(1)} %get-tuple-element.7.in_cov, f32[48,768]{1,0:T(8,128)S(1)} %get-tuple-element.8.out_cov, f32[384,768]{1,0:T(8,128)S(1)} %copy-done, ...), custom_call_target="tpu_custom_call" | custom-call | tf_op jit(solution)/shard_map/finish/pallas_call | solution.py:697
Async XLA Ops:
  0.6 147.3 %copy-start.1 = (f32[48,768]{1,0:T(8,128)S(1)}, f32[48,768]{1,0:T(8,128)}, u32[]{:S(2)}) copy-start(f32[48,768]{1,0:T(8,128)} %old_out.1) | copy-start | bytes 442372
  0.6 147.3 %copy-start = (f32[384,768]{1,0:T(8,128)S(1)}, f32[384,768]{1,0:T(8,128)}, u32[]{:S(2)}) copy-start(f32[384,768]{1,0:T(8,128)} %old_in.1) | copy-start | bytes 3538948

commit v5 on v4

--- a/solution.py
+++ b/solution.py
@@ -11,6 +11,7 @@
 factor_decay = 0.9
 MESH = pl.DeviceIdType.MESH
 CHUNKS = 3
+CROSSED = 1
 WAVES = 2
 MESSAGES = 256
 F32 = jnp.float32
@@ -553,20 +554,40 @@
     def start_other(chunk):
         own, other, across, region = ends[chunk]
         across.arrived()
-        other.start(0)
-        other.start(1)
+        if chunk >= CROSSED:
+            other.start(0)
+            other.start(1)
         pass_to_core(region(z, None, 1 - xh))
+
+    crossed = {}
+
+    def cross_over(chunk, place, name):
+        ref = ends[chunk][3](place, None, xh)
+        crossed[chunk, name] = Message(pool, ref, ref, x_far).start()
+
+    def crossed_over(chunk, place, name):
+        crossed[chunk, name].arrived()
+        pass_to_core(ends[chunk][3](place, None, 1 - xh))
 
     def forward(chunk, high):
         gather = ends[chunk][high]
         region = ends[chunk][3]
+        if high == 1 and chunk < CROSSED:
+            return
         gather.forward()
         gather.near()
         for place in (above, below):
             pass_to_core(region(place, None, xh if high == 0 else 1 - xh))
 
     def last(chunk, high):
+        if high == 1 and chunk < CROSSED:
+            crossed_over(chunk, above, "above")
+            crossed_over(chunk, below, "below")
+            crossed_over(chunk, far, "far")
+            return
         ends[chunk][high].far()
+        if chunk < CROSSED:
+            cross_over(chunk, far, "far")
         pass_to_core(ends[chunk][3](far, None, xh if high == 0 else 1 - xh))
 
     for chunk in range(CHUNKS):
@@ -578,13 +599,18 @@
             start_other(chunk - 1)
         if chunk >= 2:
             forward(chunk - 2, 1)
+    for chunk in range(CROSSED):
+        cross_over(chunk, above, "above")
+        cross_over(chunk, below, "below")
     forward(CHUNKS - 1, 0)
     start_other(CHUNKS - 1)
+    for chunk in range(CROSSED):
+        last(chunk, 0)
     if CHUNKS > 1:
         forward(CHUNKS - 2, 1)
 
     forward(CHUNKS - 1, 1)
-    for chunk in range(CHUNKS):
+    for chunk in range(CROSSED, CHUNKS):
         last(chunk, 0)
     cov_message.arrived()
     total = cov_scatter.total(xh) + cov_across[...].astype(F32)
@@ -603,7 +629,7 @@
         own.sent()
         other.sent()
         across.sent()
-    for message in crossings + to_core_last + list(scatter_basis.values()) + small + turned_core:
+    for message in list(crossed.values()) + crossings + to_core_last + list(scatter_basis.values()) + small + turned_core:
         message.sent()
     for message in list(token_messages.values()) + [column_message, grad_message, cov_message, right_message]:
         message.sent()

time: 152 us -> 146 us (0.961)
  Pallas kernels: 151 us -> 145 us
    pallas_call x1, Pallas kernels: 147 us -> 141 us  [shards(): pl.pallas_call(kernel, out_shape=(pltpu.VMEM((total, width), BF16), pltpu...]
where the time goes in v5:
time: 146 us
  Pallas kernels  145 us (99%)
    pallas_call x1, Pallas kernels, shards(): pl.pallas_call(kernel, out_shape=(pltpu.VMEM((total, width), BF16), pltpu...  141 us
    pallas_call x1, Pallas kernels, shards(): pl.pallas_call(functools.partial(finish, tokens=16 * tokens), out_shape=(...  4.15 us

profile of v5, /device:TPU:1, one launch (start us, length us, event | category | flops | bytes accessed | tf_op | source)
XLA Modules:
  0.0 145.9 jit_solution(10760285519975919894)
XLA Ops:
  0.6 0.0 copy-start.1
  0.6 0.0 copy-start
  0.7 140.9 %precondition.1 = (bf16[6144,768]{1,0:T(8,128)(2,1)S(1)}, f32[384,768]{1,0:T(8,128)S(1)}, f32[48,768]{1,0:T(8,128)S(1)}) custom-call(bf16[512,6144]{1,0:T(8,128)(2,1)} %inputs.1, bf16[512,6144]{1,0:T(8,128)(2,1)} %grads.1, bf16[384,768]{1,0:T(8,128)(2,1)} %kernel_grad.1, bf16[48,6144]{1,0:T(8,128)(2,1)} %basis_in.1, bf16[768,768]{1,0:T(8,128)(2,1)} %basis_out.1, ...), custom_call_target="tpu_custom_call" | custom-call | flops 20000000000 | bytes 40000000 | tf_op jit(solution)/shard_map/precondition/pallas_call | solution.py:699
  141.6 0.0 copy-done.1
  141.6 0.0 copy-done
  141.6 4.2 %finish.1 = (bf16[6144,768]{1,0:T(8,128)(2,1)}, f32[384,768]{1,0:T(8,128)}, f32[48,768]{1,0:T(8,128)}) custom-call(bf16[6144,768]{1,0:T(8,128)(2,1)S(1)} %get-tuple-element.6.gathered, f32[384,768]{1,0:T(8,128)S(1)} %get-tuple-element.7.in_cov, f32[48,768]{1,0:T(8,128)S(1)} %get-tuple-element.8.out_cov, f32[384,768]{1,0:T(8,128)S(1)} %copy-done, ...), custom_call_target="tpu_custom_call" | custom-call | tf_op jit(solution)/shard_map/finish/pallas_call | solution.py:723
Async XLA Ops:
  0.6 140.9 %copy-start.1 = (f32[48,768]{1,0:T(8,128)S(1)}, f32[48,768]{1,0:T(8,128)}, u32[]{:S(2)}) copy-start(f32[48,768]{1,0:T(8,128)} %old_out.1) | copy-start | bytes 442372
  0.6 140.9 %copy-start = (f32[384,768]{1,0:T(8,128)S(1)}, f32[384,768]{1,0:T(8,128)}, u32[]{:S(2)}) copy-start(f32[384,768]{1,0:T(8,128)} %old_in.1) | copy-start | bytes 3538948

commit v6 on v5

--- a/solution.py
+++ b/solution.py
@@ -518,10 +518,11 @@
     for chunk in range(CHUNKS):
         if chunk + 1 < CHUNKS:
             crosses.append(start_sum(1, (chunk + 1) * lines, lines))
+        if chunk == 1:
+            sums[1].add()
         crosses[chunk]()
-        if chunk == 1:
+        if chunk == CHUNKS - 1:
             right_scatter.add()
-            sums[1].add()
     restored_part[:, :wave] = finish_sum(sums[0])
     last_sums = sums[1:]
 

time: 146 us -> 144 us (0.986)
  Pallas kernels: 145 us -> 143 us
    pallas_call x1, Pallas kernels: 141 us -> 139 us  [shards(): pl.pallas_call(kernel, out_shape=(pltpu.VMEM((total, width), BF16), pltpu...]
where the time goes in v6:
time: 144 us
  Pallas kernels  143 us (99%)
    pallas_call x1, Pallas kernels, shards(): pl.pallas_call(kernel, out_shape=(pltpu.VMEM((total, width), BF16), pltpu...  139 us
    pallas_call x1, Pallas kernels, shards(): pl.pallas_call(functools.partial(finish, tokens=16 * tokens), out_shape=(...  4.15 us

profile of v6, /device:TPU:1, one launch (start us, length us, event | category | flops | bytes accessed | tf_op | source)
XLA Modules:
  0.0 143.7 jit_solution(2355761115767148385)
XLA Ops:
  0.6 0.0 copy-start.1
  0.6 0.0 copy-start
  0.7 138.7 %precondition.1 = (bf16[6144,768]{1,0:T(8,128)(2,1)S(1)}, f32[384,768]{1,0:T(8,128)S(1)}, f32[48,768]{1,0:T(8,128)S(1)}) custom-call(bf16[512,6144]{1,0:T(8,128)(2,1)} %inputs.1, bf16[512,6144]{1,0:T(8,128)(2,1)} %grads.1, bf16[384,768]{1,0:T(8,128)(2,1)} %kernel_grad.1, bf16[48,6144]{1,0:T(8,128)(2,1)} %basis_in.1, bf16[768,768]{1,0:T(8,128)(2,1)} %basis_out.1, ...), custom_call_target="tpu_custom_call" | custom-call | flops 20000000000 | bytes 40000000 | tf_op jit(solution)/shard_map/precondition/pallas_call | solution.py:700
  139.4 0.0 copy-done.1
  139.4 0.0 copy-done
  139.4 4.2 %finish.1 = (bf16[6144,768]{1,0:T(8,128)(2,1)}, f32[384,768]{1,0:T(8,128)}, f32[48,768]{1,0:T(8,128)}) custom-call(bf16[6144,768]{1,0:T(8,128)(2,1)S(1)} %get-tuple-element.6.gathered, f32[384,768]{1,0:T(8,128)S(1)} %get-tuple-element.7.in_cov, f32[48,768]{1,0:T(8,128)S(1)} %get-tuple-element.8.out_cov, f32[384,768]{1,0:T(8,128)S(1)} %copy-done, ...), custom_call_target="tpu_custom_call" | custom-call | tf_op jit(solution)/shard_map/finish/pallas_call | solution.py:724
Async XLA Ops:
  0.6 138.7 %copy-start.1 = (f32[48,768]{1,0:T(8,128)S(1)}, f32[48,768]{1,0:T(8,128)}, u32[]{:S(2)}) copy-start(f32[48,768]{1,0:T(8,128)} %old_out.1) | copy-start | bytes 442372
  0.6 138.7 %copy-start = (f32[384,768]{1,0:T(8,128)S(1)}, f32[384,768]{1,0:T(8,128)}, u32[]{:S(2)}) copy-start(f32[384,768]{1,0:T(8,128)} %old_in.1) | copy-start | bytes 3538948
